TPU v7x, 256 devices: a whole 4x4x8 slice. The times are simulated.
256 devices in a mesh: aux: 4 (over z_lo), ao: 64 (over z_hi, x, y, core).
Axes of the slice: x: 4, y: 4, z: 8 (z_hi: 2, z_lo: 4; z = z_hi * 4 + z_lo), core: 2. Of those that a mesh axis runs over, the one named last changes fastest.
Arguments:
- half_transformed: bfloat16 [16, 1024, 65536], P('aux', None, 'ao'), may hold values from -1.25 to 1.25
- pair_mask: int32 [512, 6], P('ao'), may hold values 0 or 1
Outputs:
- exchange_tiles: float32 [512, 12, 128, 128], P('ao', None, 'aux')
All inputs are finite; a program needn't handle non-finite values. No bound on the sum of `pair_mask` on one device may be relied on, other than what follows from the above.
Results may differ from a plain program's by a relative error of at most 0.012.
Values may be sent and summed in bfloat16 or wider, within the bound.
A program may use at most 128 MiB of HBM per device.

v0:
```python
import jax
import jax.numpy as jnp
from jax import lax
from jax.sharding import PartitionSpec as P


def from_behind(array, axis, by):
    size = lax.axis_size(axis)
    pairs = [(i, i + by) for i in range(size) if 0 <= i + by < size]
    return lax.ppermute(array, axis, pairs)


def body(half_transformed, pair_mask):
    blocks = pair_mask.shape[0]
    reach = pair_mask.shape[1]
    span = 128
    own_rows = half_transformed.reshape(-1, blocks * span)
    blank = jnp.zeros((span, span), jnp.float32)
    partner = from_behind(half_transformed[:, :, : reach * span], "ao", -1)
    partner_rows = partner.reshape(-1, reach * span)
    extended = jnp.concatenate([own_rows, partner_rows], axis=1)

    def tile_with(block, offset):
        left = extended[:, block * span : (block + 1) * span]
        right = extended[:, (block + offset) * span : (block + offset + 1) * span]
        return lax.cond(
            pair_mask[block, offset - 1] > 0,
            lambda: lax.dot_general(
                left, right, (((0,), (0,)), ((), ())), preferred_element_type=jnp.float32
            ),
            lambda: blank,
        )

    rows_of_tiles = []
    for block in range(blocks):
        rows_of_tiles.append(
            jnp.stack([tile_with(block, offset) for offset in range(1, reach + 1)], axis=0)
        )
    partials = jnp.stack(rows_of_tiles, axis=0).astype(jnp.bfloat16)
    previous = from_behind(partials[blocks - reach :], "ao", 1)
    joined = jnp.concatenate([previous, partials], axis=0)
    lowers = []
    for offset in range(reach, 0, -1):
        source = joined[reach - offset : reach - offset + blocks, offset - 1]
        lowers.append(jnp.swapaxes(source, 1, 2))
    lowers = jnp.stack(lowers, axis=1)
    stacked = jnp.concatenate([lowers, partials], axis=1).astype(jnp.float32)
    return lax.psum_scatter(
        stacked.astype(jnp.bfloat16), "aux", scatter_dimension=2, tiled=True
    ).astype(jnp.float32)


def solution(mesh):
    return jax.shard_map(
        body,
        mesh=mesh,
        in_specs=(P("aux", None, "ao"), P("ao", None)),
        out_specs=P("ao", None, "aux", None),
        check_vma=False,
    )
```

profile of v0, /device:TPU:31, one launch (start us, length us, event | category | flops | bytes accessed | tf_op | source)
XLA Modules:
  0.0 373.4 jit_solution(9589799836431864762)
XLA Ops:
  6.5 6.5 %slice.310 = bf16[4,1024,768]{2,1,0:T(8,128)(2,1)} slice(bf16[4,1024,1024]{2,1,0:T(8,128)(2,1)} %param.98), slice={[0:4], [0:1024], [0:768]} | slice | bytes 12582912 | tf_op jit(solution)/shard_map/slice | solution.py:19
  13.0 2.6 collective-permute-start
  15.6 3.4 fusion.3
  59.2 2.0 conditional.90
  59.2 2.0 convolution_bitcast_fusion.42
  76.3 17.5 %collective-permute-done = bf16[4,1024,768]{2,1,0:T(8,128)(2,1)} collective-permute-done((bf16[4,1024,768]{2,1,0:T(8,128)(2,1)}, bf16[4,1024,768]{2,1,0:T(8,128)(2,1)}, u32[]{:S(2)}, u32[]{:S(2)}) %collective-permute-start) | collective-permute-done | bytes 6291488 | tf_op jit(solution)/shard_map/ppermute | solution.py:10
  93.8 4.9 %fusion.4 = (bf16[4096,128]{1,0:T(8,128)(2,1)}, bf16[4096,128]{1,0:T(8,128)(2,1)}, bf16[4096,128]{1,0:T(8,128)(2,1)}, bf16[4096,128]{1,0:T(8,128)(2,1)}, bf16[4096,128]{1,0:T(8,128)(2,1)}) fusion(bf16[4096,768]{1,0:T(8,128)(2,1)} %bitcast.55), kind=kLoop, calls=%fused_computation.155 | loop fusion | bytes 10485760 | tf_op jit(solution)/shard_map/slice | solution.py:25
  98.8 2.3 conditional.78
  98.8 2.3 convolution_bitcast_fusion.30
  102.4 2.6 conditional.53
  102.4 2.6 convolution_bitcast_fusion.5
  106.5 2.6 conditional.58
  106.5 2.6 convolution_bitcast_fusion.10
  110.5 2.6 conditional.59
  110.5 2.6 convolution_bitcast_fusion.11
  114.5 2.6 conditional.63
  114.5 2.6 convolution_bitcast_fusion.15
  118.5 2.6 conditional.64
  118.5 2.6 convolution_bitcast_fusion.16
  124.5 2.3 conditional.68
  124.5 2.3 convolution_bitcast_fusion.20
  130.2 2.3 conditional.70
  130.2 2.3 convolution_bitcast_fusion.22
  133.9 2.3 conditional.71
  133.9 2.3 convolution_bitcast_fusion.23
  137.6 2.3 conditional.79
  137.6 2.3 convolution_bitcast_fusion.31
  141.2 2.3 conditional.80
  141.2 2.3 convolution_bitcast_fusion.32
  146.9 2.3 conditional.82
  146.9 2.3 convolution_bitcast_fusion.34
  150.6 2.3 conditional.83
  150.6 2.3 convolution_bitcast_fusion.35
  155.6 2.3 conditional.74
  155.6 2.3 convolution_bitcast_fusion.26
  161.5 2.3 conditional.77
  161.5 2.3 convolution_bitcast_fusion.29
  171.7 1.9 collective-permute-start.1
  181.1 2.7 conditional.91
  181.2 2.6 convolution_bitcast_fusion.43
  185.6 2.3 conditional.95
  185.6 2.3 convolution_bitcast_fusion.47
  189.9 1.8 conditional.88
  199.0 4.1 %constant_dynamic-update-slice_fusion.64 = (bf16[13,6,128,128]{3,2,1,0:T(8,128)(2,1)S(1)}, bf16[12,6,128,128]{3,2,1,0:T(8,128)(2,1)}, bf16[11,6,128,128]{3,2,1,0:T(8,128)(2,1)}, bf16[10,6,128,128]{3,2,1,0:T(8,128)(2,1)}) fusion(bf16[6,6,128,128]{3,2,1,0:T(8,128)(2,1)} %collective-permute-done.1), kind=kLoop, calls=%fused_computation.144 | loop fusion | bytes 5898240
  206.2 1.9 bitcast_dynamic-update-slice_fusion.15
  208.1 1.8 bitcast_dynamic-update-slice_fusion.10
  234.4 129.7 %reduce-scatter.2.cloned.1.call-done = bf16[8,12,32,128]{3,2,1,0:T(8,128)(2,1)} async-done(((bf16[8,12,128,128]{3,2,1,0:T(8,128)(2,1)}), bf16[8,12,32,128]{3,2,1,0:T(8,128)(2,1)}) %reduce-scatter.2.cloned.1.call-update) | async-done | bytes 786448 | tf_op jit(solution)/shard_map/reduce_scatter | solution.py:48
  364.1 2.5 convert_element_type.390
  (211 shorter events, 130.7 us)
Async XLA Ops:
  6.5 357.6 %reduce-scatter.2.cloned.1.call-start = ((), (), s32[]{:S(2)}) async-start(), calls=%async_computation.1 | async-start | bytes 3932160 | tf_op jit(solution)/shard_map/reduce_scatter | solution.py:48
  6.5 9.0 %copy-start.1 = (bf16[4,1024,1024]{2,1,0:T(8,128)(2,1)S(1)}, bf16[4,1024,1024]{2,1,0:T(8,128)(2,1)}, u32[]{:S(2)}) copy-start(bf16[4,1024,1024]{2,1,0:T(8,128)(2,1)} %param.98) | copy-start | bytes 25165828
  13.0 80.8 %collective-permute-start = (bf16[4,1024,768]{2,1,0:T(8,128)(2,1)}, bf16[4,1024,768]{2,1,0:T(8,128)(2,1)}, u32[]{:S(2)}, u32[]{:S(2)}) collective-permute-start(bf16[4,1024,768]{2,1,0:T(8,128)(2,1)} %slice.310), channel_id=1, source_target_pairs={{1,0},{2,1},{3,2},{4,3},{5,4},{6,5},{7,6},{8,7},{9,8},{10,9},{11,1... | collective-permute-start | bytes 18874376 | tf_op jit(solution)/shard_map/ppermute | solution.py:10
  15.6 3.4 copy-start.12
  45.2 0.6 copy-start.13
  45.8 3.5 copy-start.14
  49.3 1.8 copy-start.15
  51.0 0.6 copy-start.16
  51.1 4.0 %copy-start.17 = (bf16[1,128,128]{2,1,0:T(8,128)(2,1)}, bf16[1,128,128]{2,1,0:T(8,128)(2,1)S(1)}, u32[]{:S(2)}) copy-start(bf16[1,128,128]{2,1,0:T(8,128)(2,1)S(1)} %get-tuple-element.581) | copy-start | bytes 98308
  53.3 1.8 copy-start.18
  55.1 0.6 copy-start.19
  55.2 4.0 %copy-start.20 = (bf16[1,128,128]{2,1,0:T(8,128)(2,1)}, bf16[1,128,128]{2,1,0:T(8,128)(2,1)S(1)}, u32[]{:S(2)}) copy-start(bf16[1,128,128]{2,1,0:T(8,128)(2,1)S(1)} %get-tuple-element.575) | copy-start | bytes 98308
  57.4 1.8 copy-start.21
  59.1 2.1 copy-start.22
  59.2 2.1 copy-start.23
  61.2 0.6 copy-start.24
  171.7 23.5 %collective-permute-start.1 = (bf16[6,6,128,128]{3,2,1,0:T(8,128)(2,1)}, bf16[6,6,128,128]{3,2,1,0:T(8,128)(2,1)}, u32[]{:S(2)}, u32[]{:S(2)}) collective-permute-start(bf16[6,6,128,128]{3,2,1,0:T(8,128)(2,1)} %bitcast_dynamic-update-slice_fusion.1), channel_id=1, source_target_pairs={{0,1},{1,2},{2,3},{3,4},{4,5},{5,6},{6,7},{7,8},{8,9},{9,10},{10,1... | collective-permute-start | bytes 3538952 | tf_op jit(solution)/shard_map/ppermute | solution.py:10
  187.9 1.3 copy-start
  189.8 3.6 copy-start.3
  189.8 3.6 copy-start.29
  189.8 3.6 copy-start.30
  189.8 4.5 %copy-start.7 = (bf16[6,128,128]{2,1,0:T(8,128)(2,1)S(1)}, bf16[6,128,128]{2,1,0:T(8,128)(2,1)}, u32[]{:S(2)}) copy-start(bf16[6,128,128]{2,1,0:T(8,128)(2,1)} %constant_dynamic-update-slice_fusion.48) | copy-start | bytes 589828
  189.8 4.5 %copy-start.25 = (bf16[1,128,128]{2,1,0:T(8,128)(2,1)S(1)}, bf16[1,128,128]{2,1,0:T(8,128)(2,1)}, u32[]{:S(2)}) copy-start(bf16[1,128,128]{2,1,0:T(8,128)(2,1)} %get-tuple-element.617) | copy-start | bytes 98308
  189.8 4.5 %copy-start.26 = (bf16[1,128,128]{2,1,0:T(8,128)(2,1)S(1)}, bf16[1,128,128]{2,1,0:T(8,128)(2,1)}, u32[]{:S(2)}) copy-start(bf16[1,128,128]{2,1,0:T(8,128)(2,1)} %get-tuple-element.618) | copy-start | bytes 98308
  189.9 4.5 %copy-start.27 = (bf16[1,128,128]{2,1,0:T(8,128)(2,1)S(1)}, bf16[1,128,128]{2,1,0:T(8,128)(2,1)}, u32[]{:S(2)}) copy-start(bf16[1,128,128]{2,1,0:T(8,128)(2,1)} %get-tuple-element.619) | copy-start | bytes 98308
  189.9 4.5 %copy-start.28 = (bf16[1,128,128]{2,1,0:T(8,128)(2,1)S(1)}, bf16[1,128,128]{2,1,0:T(8,128)(2,1)}, u32[]{:S(2)}) copy-start(bf16[1,128,128]{2,1,0:T(8,128)(2,1)} %get-tuple-element.620) | copy-start | bytes 98308
  194.3 2.9 copy-start.4
  195.2 2.0 copy-start.8
  199.0 4.1 %copy-start.5 = (bf16[6,128,128]{2,1,0:T(8,128)(2,1)S(1)}, bf16[6,128,128]{2,1,0:T(8,128)(2,1)}, u32[]{:S(2)}) copy-start(bf16[6,128,128]{2,1,0:T(8,128)(2,1)} %copy-done.4) | copy-start | bytes 589828
  199.0 5.1 %copy-start.9 = (bf16[6,128,128]{2,1,0:T(8,128)(2,1)S(1)}, bf16[6,128,128]{2,1,0:T(8,128)(2,1)}, u32[]{:S(2)}) copy-start(bf16[6,128,128]{2,1,0:T(8,128)(2,1)} %copy-done.8) | copy-start | bytes 589828
  224.6 5.1 %copy-start.6 = (bf16[6,128,128]{2,1,0:T(8,128)(2,1)S(1)}, bf16[6,128,128]{2,1,0:T(8,128)(2,1)}, u32[]{:S(2)}) copy-start(bf16[6,128,128]{2,1,0:T(8,128)(2,1)} %copy-done.4) | copy-start | bytes 589828
  224.6 5.1 %copy-start.10 = (bf16[6,128,128]{2,1,0:T(8,128)(2,1)S(1)}, bf16[6,128,128]{2,1,0:T(8,128)(2,1)}, u32[]{:S(2)}) copy-start(bf16[6,128,128]{2,1,0:T(8,128)(2,1)} %copy-done.8) | copy-start | bytes 589828
  225.6 7.0 %copy-start.11 = (bf16[6,128,128]{2,1,0:T(8,128)(2,1)S(1)}, bf16[6,128,128]{2,1,0:T(8,128)(2,1)}, u32[]{:S(2)}) copy-start(bf16[6,128,128]{2,1,0:T(8,128)(2,1)} %constant_dynamic-update-slice_fusion.30) | copy-start | bytes 589828
  232.7 1.7 copy-start.2
Sparse Core Ops, SparseCore 0:
  234.6 129.5 reduce-scatter.1
where the time goes:
time: 375 us; the launch traced here: 373 us
  waiting for transfers between devices  147 us (39%)
  local copies, waits for them, and re-layouts  114 us (30%)
  matrix products  59.1 us (16%)
  between operations  44.2 us (12%)
  starting transfers between devices  4.48 us (1%)
    reduce_scatter x1, waiting for transfers between devices, body(): lax.psum_scatter(stacked.astype(jnp.bfloat16), 'aux', scatter_dimension=2...  130 us
    unnamed x127, local copies, waits for them, and re-layouts  65.9 us
    dot_general x28, matrix products, tile_with(): lax.dot_general(left, right, (((0,), (0,)), ((), ())), preferred_element_...  59.1 us
    ppermute x2, waiting for transfers between devices, from_behind(): return lax.ppermute(array, axis, pairs)  17.5 us
    another operation x28, local copies, waits for them, and re-layouts, body(): jnp.stack([tile_with(block, offset) for offset in range(1, reach + 1)], a...  15.2 us
    another operation x10, local copies, waits for them, and re-layouts, body(): lowers = jnp.stack(lowers, axis=1)  14.6 us
  transfers between devices with their start and end apart: 3, of which 2 were waited for; matrix products, arithmetic and copies ran while one was open for 13% of the time, Pallas kernels for 0%

commit v1 on v0

v1 whole, which is shorter than its diff:
```python
import functools

import jax
import jax.numpy as jnp
from jax import lax
from jax.experimental import pallas as pl
from jax.experimental.pallas import tpu as pltpu
from jax.sharding import PartitionSpec as P

MESH = pl.DeviceIdType.MESH
BS = 128
W = 6
NBLK = 8
AUX = 4
SL = BS // AUX
KC = 512

INNER = [(i, j) for j in range(1, NBLK) for i in range(max(0, j - W), j)]
INNER_M = [1, 3, 5, 7]
INNER_OFF = [0, 1, 4, 9]
RIGHT = [[(i, b) for i in range(b, W - b)] for b in range(3)]
LEFT = [[(b, j) for j in range(b + 1, W - b)] for b in range(3)]
LO = [1, 2, 3]
HI = [8, 7, 6]


def groups_of(count):
    return (count + 3) // 4


N_IN = len(INNER)
G_IN = groups_of(N_IN)
T0 = [0, N_IN]
for b in range(3):
    T0.append(T0[-1] + len(RIGHT[b]) + len(LEFT[b]))
N_ALL = T0[-1]
GR = [0]
GL = [0]
for b in range(3):
    GR.append(GR[-1] + groups_of(len(RIGHT[b])))
    GL.append(GL[-1] + groups_of(len(LEFT[b])))


def kernel(
    x_hbm, mask_ref, out_ref,
    x, xt, hal, acc, part, rbuf, ts_in, ts_r, ts_l, tr_in, tr_r, tr_l, mask_own, mask_prev,
    load_sem, hs, hr, ms, mr, s1s, s1r, s2s, s2r, crs, crr, cls, clr,
):
    rows = x.shape[0]
    chunks = rows // KC
    n = lax.axis_index("ao")
    a = lax.axis_index("aux")
    n_ao = lax.axis_size("ao")
    has_left = n > 0
    has_right = n < n_ao - 1
    left = jnp.maximum(n - 1, 0)
    right = jnp.minimum(n + 1, n_ao - 1)

    def aux_peer(r):
        return lax.rem(a + r, AUX)

    barrier = pltpu.get_barrier_semaphore()
    for r in range(1, AUX):
        pl.semaphore_signal(barrier, 1, device_id={"aux": aux_peer(r)}, device_id_type=MESH)

    @pl.when(has_left)
    def _():
        for b in range(AUX):
            pl.semaphore_signal(barrier, 1, device_id={"ao": left, "aux": b}, device_id_type=MESH)

    @pl.when(has_right)
    def _():
        for b in range(AUX):
            pl.semaphore_signal(barrier, 1, device_id={"ao": right, "aux": b}, device_id_type=MESH)

    def load(c):
        piece = pl.ds(pl.multiple_of(c * KC, KC), KC)
        return pltpu.make_async_copy(x_hbm.at[piece], x.at[piece], load_sem.at[c])

    for c in range(chunks):
        load(c).start()
    mask_own[...] = jnp.zeros_like(mask_own)
    mask_own[:, 0:W] = mask_ref[...]

    pl.semaphore_wait(
        barrier, AUX - 1 + AUX * (has_left.astype(jnp.int32) + has_right.astype(jnp.int32)))

    def to_left(b):
        return pltpu.make_async_remote_copy(
            x_hbm.at[:, pl.ds(b * BS, BS)], hal.at[b, :, pl.ds(0, BS)],
            hs.at[0, b], hr.at[0, b], device_id={"ao": left}, device_id_type=MESH)

    def to_right(b):
        return pltpu.make_async_remote_copy(
            x_hbm.at[:, pl.ds((NBLK - 1 - b) * BS, BS)], hal.at[b, :, pl.ds(BS, BS)],
            hs.at[1, b], hr.at[1, b], device_id={"ao": right}, device_id_type=MESH)

    mask_copy = pltpu.make_async_remote_copy(
        mask_own, mask_prev, ms, mr, device_id={"ao": right}, device_id_type=MESH)

    @pl.when(has_right)
    def _():
        mask_copy.start()

    for b in range(3):
        @pl.when(has_left)
        def _():
            to_left(b).start()

        @pl.when(has_right)
        def _():
            to_right(b).start()

    @pl.when(jnp.logical_not(has_left))
    def _():
        hal[:, :, BS:] = jnp.zeros((3, rows, BS), hal.dtype)
        tr_r[...] = jnp.zeros_like(tr_r)
        mask_prev[...] = jnp.zeros_like(mask_prev)

    @pl.when(jnp.logical_not(has_right))
    def _():
        hal[:, :, :BS] = jnp.zeros((3, rows, BS), hal.dtype)
        tr_l[...] = jnp.zeros_like(tr_l)

    acc[...] = jnp.zeros_like(acc)

    def inner_step(c, carry):
        load(c).wait()
        piece = pl.ds(pl.multiple_of(c * KC, KC), KC)
        for b in range(NBLK):
            xt[c, b * BS:(b + 1) * BS, :] = x[piece, b * BS:(b + 1) * BS].T
        for q in range(4):
            lhs = xt[c, 0:INNER_M[q] * BS, :]
            rhs = x[piece, 2 * q * BS:(2 * q + 2) * BS]
            where = slice(INNER_OFF[q] * BS, (INNER_OFF[q] + INNER_M[q]) * BS)
            acc[where, :] += jnp.dot(lhs, rhs, preferred_element_type=jnp.float32)
        return carry

    lax.fori_loop(0, chunks, inner_step, 0)

    def put(tile, keep, t):
        scaled = tile * (keep > 0).astype(jnp.float32)
        part[:, t] = scaled.astype(part.dtype).reshape(AUX, SL, BS)

    for t, (i, j) in enumerate(INNER):
        row = (INNER_OFF[j // 2] + i) * BS
        col = (j % 2) * BS
        put(acc[row:row + BS, col:col + BS], mask_own[i:i + 1, j - i - 1:j - i], t)

    def send1(k, r):
        span = pl.ds(T0[k], T0[k + 1] - T0[k])
        return pltpu.make_async_remote_copy(
            part.at[aux_peer(r), span], rbuf.at[r - 1, span],
            s1s.at[k, r - 1], s1r.at[k, r - 1], device_id={"aux": aux_peer(r)}, device_id_type=MESH)

    for r in range(1, AUX):
        send1(0, r).start()

    def cross(b):
        @pl.when(has_right)
        def _():
            to_left(b).wait_recv()

        @pl.when(has_left)
        def _():
            to_right(b).wait_recv()

        if b == 0:
            @pl.when(has_left)
            def _():
                mask_copy.wait_recv()

        lo, size = LO[b] * BS, (HI[b] - LO[b]) * BS
        acc[0:size, :] = jnp.zeros((size, 2 * BS), jnp.float32)

        def step(c, carry):
            piece = pl.ds(pl.multiple_of(c * KC, KC), KC)
            acc[0:size, :] += jnp.dot(
                xt[c, lo:lo + size, :], hal[b, piece, :], preferred_element_type=jnp.float32)
            return carry

        lax.fori_loop(0, chunks, step, 0)
        t = T0[b + 1]
        for i, j in RIGHT[b]:
            own = NBLK - 1 - i
            row = (own - LO[b]) * BS
            put(acc[row:row + BS, 0:BS], mask_own[own:own + 1, i + j:i + j + 1], t)
            t += 1
        for i, j in LEFT[b]:
            row = (j - LO[b]) * BS
            far = NBLK - 1 - i
            put(acc[row:row + BS, BS:2 * BS], mask_prev[far:far + 1, i + j:i + j + 1], t)
            t += 1
        for r in range(1, AUX):
            send1(b + 1, r).start()

    def total(t):
        value = part[a, t].astype(jnp.float32)
        for r in range(1, AUX):
            value = value + rbuf[r - 1, t].astype(jnp.float32)
        return value

    def turn(values, ts, g):
        values = values + [jnp.zeros((SL, BS), jnp.float32)] * (4 - len(values))
        ts[:, g] = jnp.concatenate(values, axis=0).T.astype(ts.dtype).reshape(AUX, SL, BS)

    def sums(t0, places, ts, g0):
        for g in range(groups_of(len(places))):
            values = []
            for u, (m, e) in enumerate(places[4 * g:4 * g + 4]):
                value = total(t0 + 4 * g + u)
                out_ref[m, e] = value
                values.append(value)
            turn(values, ts, g0 + g)

    def send_in(r):
        return pltpu.make_async_remote_copy(
            ts_in.at[aux_peer(r)], tr_in.at[a], s2s.at[r - 1], s2r.at[r - 1],
            device_id={"aux": aux_peer(r)}, device_id_type=MESH)

    def send_r(b, to):
        span = pl.ds(GR[b], GR[b + 1] - GR[b])
        return pltpu.make_async_remote_copy(
            ts_r.at[to, span], tr_r.at[a, span], crs.at[b, to], crr.at[b, a],
            device_id={"ao": right, "aux": to}, device_id_type=MESH)

    def send_l(b, to):
        span = pl.ds(GL[b], GL[b + 1] - GL[b])
        return pltpu.make_async_remote_copy(
            ts_l.at[to, span], tr_l.at[a, span], cls.at[b, to], clr.at[b, a],
            device_id={"ao": left, "aux": to}, device_id_type=MESH)

    def got_r(b, source):
        span = pl.ds(GR[b], GR[b + 1] - GR[b])
        return pltpu.make_async_remote_copy(
            ts_r.at[source, span], tr_r.at[source, span], crs.at[b, source], crr.at[b, source],
            device_id={"ao": left, "aux": source}, device_id_type=MESH)

    def got_l(b, source):
        span = pl.ds(GL[b], GL[b + 1] - GL[b])
        return pltpu.make_async_remote_copy(
            ts_l.at[source, span], tr_l.at[source, span], cls.at[b, source], clr.at[b, source],
            device_id={"ao": right, "aux": source}, device_id_type=MESH)

    def inner_sums():
        for r in range(1, AUX):
            send1(0, r).wait_recv()
        sums(0, [(i, W + j - i - 1) for i, j in INNER], ts_in, 0)
        tr_in[a] = ts_in[a]
        for r in range(1, AUX):
            send_in(r).start()

    def cross_sums(b):
        for r in range(1, AUX):
            send1(b + 1, r).wait_recv()
        t = T0[b + 1]
        sums(t, [(NBLK - 1 - i, W + i + j) for i, j in RIGHT[b]], ts_r, GR[b])

        @pl.when(has_right)
        def _():
            for to in range(AUX):
                send_r(b, to).start()

        sums(t + len(RIGHT[b]), [(j, W - 1 - i - j) for i, j in LEFT[b]], ts_l, GL[b])

        @pl.when(has_left)
        def _():
            for to in range(AUX):
                send_l(b, to).start()

    def place(tr, g0, places):
        for u, (m, e) in enumerate(places):
            g, v = g0 + u // 4, u % 4
            pieces = [tr[source, g, :, v * SL:(v + 1) * SL].astype(jnp.float32) for source in range(AUX)]
            out_ref[m, e] = jnp.concatenate(pieces, axis=1)

    def inner_place():
        for r in range(1, AUX):
            send_in(r).wait_recv()
        place(tr_in, 0, [(j, W - (j - i)) for i, j in INNER])

    def cross_place(b):
        @pl.when(has_left)
        def _():
            for source in range(AUX):
                got_r(b, source).wait_recv()

        place(tr_r, GR[b], [(j, W - 1 - i - j) for i, j in RIGHT[b]])

        @pl.when(has_right)
        def _():
            for source in range(AUX):
                got_l(b, source).wait_recv()

        place(tr_l, GL[b], [(NBLK - 1 - i, W + i + j) for i, j in LEFT[b]])

    cross(0)
    cross(1)
    inner_sums()
    cross_sums(0)
    cross(2)
    cross_sums(1)
    inner_place()
    cross_place(0)
    cross_sums(2)
    cross_place(1)
    cross_place(2)

    for k in range(4):
        for r in range(1, AUX):
            send1(k, r).wait_send()
    for r in range(1, AUX):
        send_in(r).wait_send()

    @pl.when(has_right)
    def _():
        mask_copy.wait_send()
        for b in range(3):
            to_right(b).wait_send()
            for to in range(AUX):
                send_r(b, to).wait_send()

    @pl.when(has_left)
    def _():
        for b in range(3):
            to_left(b).wait_send()
            for to in range(AUX):
                send_l(b, to).wait_send()


def body(half_transformed, pair_mask):
    flat = half_transformed.reshape(-1, NBLK * BS)
    rows = flat.shape[0]
    bf16 = jnp.bfloat16
    dma = pltpu.SemaphoreType.DMA
    return pl.pallas_call(
        kernel,
        out_shape=jax.ShapeDtypeStruct((NBLK, 2 * W, SL, BS), jnp.float32),
        in_specs=[pl.BlockSpec(memory_space=pl.ANY), pl.BlockSpec(memory_space=pltpu.VMEM)],
        out_specs=pl.BlockSpec(memory_space=pltpu.VMEM),
        scratch_shapes=[
            pltpu.VMEM((rows, NBLK * BS), bf16),
            pltpu.VMEM((rows // KC, NBLK * BS, KC), bf16),
            pltpu.VMEM((3, rows, 2 * BS), bf16),
            pltpu.VMEM((sum(INNER_M) * BS, 2 * BS), jnp.float32),
            pltpu.VMEM((AUX, N_ALL, SL, BS), bf16),
            pltpu.VMEM((AUX - 1, N_ALL, SL, BS), bf16),
            pltpu.VMEM((AUX, G_IN, SL, BS), bf16),
            pltpu.VMEM((AUX, GR[3], SL, BS), bf16),
            pltpu.VMEM((AUX, GL[3], SL, BS), bf16),
            pltpu.VMEM((AUX, G_IN, SL, BS), bf16),
            pltpu.VMEM((AUX, GR[3], SL, BS), bf16),
            pltpu.VMEM((AUX, GL[3], SL, BS), bf16),
            pltpu.VMEM((NBLK, BS), jnp.int32),
            pltpu.VMEM((NBLK, BS), jnp.int32),
            dma((rows // KC,)),
            dma((2, 3)), dma((2, 3)),
            dma, dma,
            dma((4, AUX - 1)), dma((4, AUX - 1)),
            dma((AUX - 1,)), dma((AUX - 1,)),
            dma((3, AUX)), dma((3, AUX)),
            dma((3, AUX)), dma((3, AUX)),
        ],
        compiler_params=pltpu.CompilerParams(
            collective_id=0, has_side_effects=True, vmem_limit_bytes=48 << 20),
        cost_estimate=pl.CostEstimate(flops=8 << 30, bytes_accessed=16 << 20, transcendentals=0),
    )(flat, pair_mask)


def solution(mesh):
    return jax.shard_map(
        body,
        mesh=mesh,
        in_specs=(P("aux", None, "ao"), P("ao", None)),
        out_specs=P("ao", None, "aux", None),
        check_vma=False,
    )
```

time: 375 us -> 122 us (0.33)
  waiting for transfers between devices: 147 us -> 0 us
  Pallas kernels: 0 us -> 120 us
  local copies, waits for them, and re-layouts: 114 us -> 1.83 us
  matrix products: 59.1 us -> 0 us
  between operations: 44.2 us -> 0.01 us
  starting transfers between devices: 4.48 us -> 0 us
    reduce_scatter x1 -> x0, waiting for transfers between devices: 130 us -> none  [body(): lax.psum_scatter(stacked.astype(jnp.bfloat16), 'aux', scatter_dimension=2...]
    pallas_call x0 -> x1, Pallas kernels: none -> 120 us  [body(): pl.pallas_call(kernel, out_shape=jax.ShapeDtypeStruct((NBLK, 2 * W, SL, B...]
    unnamed x127 -> x3, local copies, waits for them, and re-layouts: 65.9 us -> 1.83 us
    dot_general x28 -> x0, matrix products: 59.1 us -> none  [tile_with(): lax.dot_general(left, right, (((0,), (0,)), ((), ())), preferred_element_...]
    another operation x39 -> x0, local copies, waits for them, and re-layouts: 31.5 us -> none  [the longest x28 15.2 us: body(): jnp.stack([tile_with(block, offset) for offset in range(1, reach + 1)], a...]
    ppermute x2 -> x0, waiting for transfers between devices: 17.5 us -> none  [from_behind(): return lax.ppermute(array, axis, pairs)]
    slice x6 -> x0, local copies, waits for them, and re-layouts: 16.9 us -> none  [the longest x1 6.46 us: body(): partner = from_behind(half_transformed[:, :, :reach * span], 'ao', -1)]
    ppermute x2 -> x0, starting transfers between devices: 4.48 us -> none  [from_behind(): return lax.ppermute(array, axis, pairs)]
  transfers between devices with their start and end apart: 3 -> 0, of which waited for: 2 -> 0; matrix products, arithmetic and copies ran while one was open for 13% -> 0% of each run, Pallas kernels for 0% -> 0%
where the time goes in v1:
time: 122 us
  Pallas kernels  120 us (98%)
  local copies, waits for them, and re-layouts  1.83 us (2%)
    pallas_call x1, Pallas kernels, body(): pl.pallas_call(kernel, out_shape=jax.ShapeDtypeStruct((NBLK, 2 * W, SL, B...  120 us

profile of v1, /device:TPU:31, one launch (start us, length us, event | category | flops | bytes accessed | tf_op | source)
XLA Modules:
  0.0 121.8 jit_solution(4578945397170618148)
XLA Ops:
  0.0 0.0 copy-start
  0.0 0.7 copy-done
  0.7 120.0 %shard_map.28 = f32[8,12,32,128]{3,2,1,0:T(8,128)S(1)} custom-call(bf16[4096,1024]{1,0:T(8,128)(2,1)} %bitcast.1, s32[8,6]{1,0:T(8,128)S(1)} %copy-done), custom_call_target="tpu_custom_call" | custom-call | flops 8589934592 | bytes 16777216 | tf_op jit(solution)/shard_map/pallas_call | solution.py:336
  120.7 1.1 copy.4
Async XLA Ops:
  0.0 0.7 copy-start

commit v2 on v1

--- a/solution.py
+++ b/solution.py
@@ -14,6 +14,8 @@
 AUX = 4
 SL = BS // AUX
 KC = 512
+SEAM = 31
+RELAY = [7, 15, 0]
 
 INNER = [(i, j) for j in range(1, NBLK) for i in range(max(0, j - W), j)]
 INNER_M = [1, 3, 5, 7]
@@ -43,14 +45,17 @@
 
 def kernel(
     x_hbm, mask_ref, out_ref,
-    x, xt, hal, acc, part, rbuf, ts_in, ts_r, ts_l, tr_in, tr_r, tr_l, mask_own, mask_prev,
-    load_sem, hs, hr, ms, mr, s1s, s1r, s2s, s2r, crs, crr, cls, clr,
+    x, xt, hal, rel, acc, part, rbuf, ts_in, ts_r, ts_l, tr_in, tr_r, tr_l, mask_own, mask_prev,
+    load_sem, hs, hr, ss, sr, rs, rr, ms, mr, s1s, s1r, s2s, s2r, crs, crr, cls, clr,
 ):
     rows = x.shape[0]
     chunks = rows // KC
     n = lax.axis_index("ao")
     a = lax.axis_index("aux")
     n_ao = lax.axis_size("ao")
+    fwd = n <= SEAM
+    at_seam = (n == SEAM) | (n == SEAM + 1)
+    last = n_ao - 1
     has_left = n > 0
     has_right = n < n_ao - 1
     left = jnp.maximum(n - 1, 0)
@@ -73,6 +78,29 @@
         for b in range(AUX):
             pl.semaphore_signal(barrier, 1, device_id={"ao": right, "aux": b}, device_id_type=MESH)
 
+    quarter = rows // AUX
+
+    def relay_of(p):
+        return jnp.where(fwd, RELAY[p - 1], last - RELAY[p - 1])
+
+    def is_relay(p):
+        return n == relay_of(p)
+
+    relay_to = jnp.where(fwd, SEAM + 1, SEAM)
+    relay_from = jnp.where(fwd, SEAM, SEAM + 1)
+    extra = jnp.where(at_seam, AUX - 1, 0)
+    for p in range(1, AUX):
+        extra += jnp.where(is_relay(p), 1, 0)
+
+        @pl.when(is_relay(p))
+        def _():
+            pl.semaphore_signal(barrier, 1, device_id={"ao": relay_from}, device_id_type=MESH)
+
+        @pl.when(at_seam)
+        def _():
+            other = jnp.where(fwd, last - RELAY[p - 1], RELAY[p - 1])
+            pl.semaphore_signal(barrier, 1, device_id={"ao": other}, device_id_type=MESH)
+
     def load(c):
         piece = pl.ds(pl.multiple_of(c * KC, KC), KC)
         return pltpu.make_async_copy(x_hbm.at[piece], x.at[piece], load_sem.at[c])
@@ -83,7 +111,7 @@
     mask_own[:, 0:W] = mask_ref[...]
 
     pl.semaphore_wait(
-        barrier, AUX - 1 + AUX * (has_left.astype(jnp.int32) + has_right.astype(jnp.int32)))
+        barrier, AUX - 1 + AUX * (has_left.astype(jnp.int32) + has_right.astype(jnp.int32)) + extra)
 
     def to_left(b):
         return pltpu.make_async_remote_copy(
@@ -95,6 +123,37 @@
             x_hbm.at[:, pl.ds((NBLK - 1 - b) * BS, BS)], hal.at[b, :, pl.ds(BS, BS)],
             hs.at[1, b], hr.at[1, b], device_id={"ao": right}, device_id_type=MESH)
 
+    def seam_span(p, lanes):
+        return (pl.ds(p * quarter, quarter), pl.ds(pl.multiple_of(lanes, BS), BS))
+
+    def seam_out(b, p):
+        source = x_hbm.at[seam_span(p, jnp.where(fwd, (NBLK - 1 - b) * BS, b * BS))]
+        if p == 0:
+            return pltpu.make_async_remote_copy(
+                source, hal.at[(b,) + seam_span(p, jnp.where(fwd, BS, 0))],
+                ss.at[p, b], sr.at[p, b], device_id={"ao": relay_to}, device_id_type=MESH)
+        return pltpu.make_async_remote_copy(
+            source, rel.at[b], ss.at[p, b], rr.at[b], device_id={"ao": relay_of(p)}, device_id_type=MESH)
+
+    def relay_out(b, p):
+        return pltpu.make_async_remote_copy(
+            rel.at[b], hal.at[(b,) + seam_span(p, jnp.where(fwd, BS, 0))],
+            rs.at[b], sr.at[p, b], device_id={"ao": relay_to}, device_id_type=MESH)
+
+    def seam_in(b, p):
+        return pltpu.make_async_remote_copy(
+            rel.at[b], hal.at[(b,) + seam_span(p, jnp.where(fwd, 0, BS))],
+            rs.at[b], sr.at[p, b], device_id={"ao": relay_to}, device_id_type=MESH)
+
+    def relay(b):
+        for p in range(1, AUX):
+            @pl.when(is_relay(p))
+            def _():
+                seam_out(b, p).wait_recv()
+                relay_out(b, p).start()
+
+    near_left = has_left & (n != SEAM + 1)
+    near_right = has_right & (n != SEAM)
     mask_copy = pltpu.make_async_remote_copy(
         mask_own, mask_prev, ms, mr, device_id={"ao": right}, device_id_type=MESH)
 
@@ -103,13 +162,18 @@
         mask_copy.start()
 
     for b in range(3):
-        @pl.when(has_left)
+        @pl.when(near_left)
         def _():
             to_left(b).start()
 
-        @pl.when(has_right)
+        @pl.when(near_right)
         def _():
             to_right(b).start()
+
+        @pl.when(at_seam)
+        def _():
+            for p in (1, 3, 2, 0):
+                seam_out(b, p).start()
 
     @pl.when(jnp.logical_not(has_left))
     def _():
@@ -137,6 +201,7 @@
         return carry
 
     lax.fori_loop(0, chunks, inner_step, 0)
+    relay(0)
 
     def put(tile, keep, t):
         scaled = tile * (keep > 0).astype(jnp.float32)
@@ -157,13 +222,18 @@
         send1(0, r).start()
 
     def cross(b):
-        @pl.when(has_right)
+        @pl.when(near_right)
         def _():
             to_left(b).wait_recv()
 
-        @pl.when(has_left)
+        @pl.when(near_left)
         def _():
             to_right(b).wait_recv()
+
+        @pl.when(at_seam)
+        def _():
+            for p in range(AUX):
+                seam_in(b, p).wait_recv()
 
         if b == 0:
             @pl.when(has_left)
@@ -294,7 +364,9 @@
 
         place(tr_l, GL[b], [(NBLK - 1 - i, W + i + j) for i, j in LEFT[b]])
 
+    relay(1)
     cross(0)
+    relay(2)
     cross(1)
     inner_sums()
     cross_sums(0)
@@ -316,16 +388,33 @@
     def _():
         mask_copy.wait_send()
         for b in range(3):
-            to_right(b).wait_send()
             for to in range(AUX):
                 send_r(b, to).wait_send()
 
     @pl.when(has_left)
     def _():
         for b in range(3):
-            to_left(b).wait_send()
             for to in range(AUX):
                 send_l(b, to).wait_send()
+
+    for b in range(3):
+        @pl.when(near_right)
+        def _():
+            to_right(b).wait_send()
+
+        @pl.when(near_left)
+        def _():
+            to_left(b).wait_send()
+
+        @pl.when(at_seam)
+        def _():
+            for p in range(AUX):
+                seam_out(b, p).wait_send()
+
+        for p in range(1, AUX):
+            @pl.when(is_relay(p))
+            def _():
+                relay_out(b, p).wait_send()
 
 
 def body(half_transformed, pair_mask):
@@ -342,6 +431,7 @@
             pltpu.VMEM((rows, NBLK * BS), bf16),
             pltpu.VMEM((rows // KC, NBLK * BS, KC), bf16),
             pltpu.VMEM((3, rows, 2 * BS), bf16),
+            pltpu.VMEM((3, rows // AUX, BS), bf16),
             pltpu.VMEM((sum(INNER_M) * BS, 2 * BS), jnp.float32),
             pltpu.VMEM((AUX, N_ALL, SL, BS), bf16),
             pltpu.VMEM((AUX - 1, N_ALL, SL, BS), bf16),
@@ -355,6 +445,7 @@
             pltpu.VMEM((NBLK, BS), jnp.int32),
             dma((rows // KC,)),
             dma((2, 3)), dma((2, 3)),
+            dma((AUX, 3)), dma((AUX, 3)), dma((3,)), dma((3,)),
             dma, dma,
             dma((4, AUX - 1)), dma((4, AUX - 1)),
             dma((AUX - 1,)), dma((AUX - 1,)),

time: 122 us -> 81.4 us (0.67)
  Pallas kernels: 120 us -> 78.8 us
    pallas_call x1, Pallas kernels: 120 us -> 78.8 us  [body(): pl.pallas_call(kernel, out_shape=jax.ShapeDtypeStruct((NBLK, 2 * W, SL, B...]
where the time goes in v2:
time: 81.4 us; the launch traced here: 80.7 us
  Pallas kernels  78.8 us (97%)
  local copies, waits for them, and re-layouts  1.83 us (2%)
    pallas_call x1, Pallas kernels, body(): pl.pallas_call(kernel, out_shape=jax.ShapeDtypeStruct((NBLK, 2 * W, SL, B...  78.8 us
    unnamed x3, local copies, waits for them, and re-layouts  1.83 us

profile of v2, /device:TPU:31, one launch (start us, length us, event | category | flops | bytes accessed | tf_op | source)
XLA Modules:
  0.0 80.7 jit_solution(2770685913795165287)
XLA Ops:
  0.0 0.0 copy-start
  0.0 0.7 copy-done
  0.7 78.8 %shard_map.28 = f32[8,12,32,128]{3,2,1,0:T(8,128)S(1)} custom-call(bf16[4096,1024]{1,0:T(8,128)(2,1)} %bitcast.1, s32[8,6]{1,0:T(8,128)S(1)} %copy-done), custom_call_target="tpu_custom_call" | custom-call | flops 8589934592 | bytes 16777216 | tf_op jit(solution)/shard_map/pallas_call | solution.py:425
  79.5 1.1 %copy.4 = f32[8,12,32,128]{3,2,1,0:T(8,128)} copy(f32[8,12,32,128]{3,2,1,0:T(8,128)S(1)} %shard_map.28) | data formatting | bytes 3145728
Async XLA Ops:
  0.0 0.7 copy-start

commit v3 on v2

--- a/solution.py
+++ b/solution.py
@@ -13,7 +13,7 @@
 NBLK = 8
 AUX = 4
 SL = BS // AUX
-KC = 512
+KC = 1024
 SEAM = 31
 RELAY = [7, 15, 0]
 
@@ -30,23 +30,27 @@
     return (count + 3) // 4
 
 
-N_IN = len(INNER)
-G_IN = groups_of(N_IN)
-T0 = [0, N_IN]
+EARLY = 15
+INNER_PART = [INNER[:EARLY], INNER[EARLY:]]
+T0 = [0, EARLY, len(INNER)]
 for b in range(3):
     T0.append(T0[-1] + len(RIGHT[b]) + len(LEFT[b]))
 N_ALL = T0[-1]
+TAIL = T0[4]
+GI = [0, groups_of(EARLY), groups_of(EARLY) + groups_of(len(INNER) - EARLY)]
 GR = [0]
 GL = [0]
-for b in range(3):
+for b in range(2):
     GR.append(GR[-1] + groups_of(len(RIGHT[b])))
     GL.append(GL[-1] + groups_of(len(LEFT[b])))
 
 
 def kernel(
     x_hbm, mask_ref, out_ref,
-    x, xt, hal, rel, acc, part, rbuf, ts_in, ts_r, ts_l, tr_in, tr_r, tr_l, mask_own, mask_prev,
-    load_sem, hs, hr, ss, sr, rs, rr, ms, mr, s1s, s1r, s2s, s2r, crs, crr, cls, clr,
+    x, xt, hal, rel, acc, part, own_sum, far_sum, far_out, far_in, tail_in,
+    ts_in, ts_r, ts_l, tr_in, tr_r, tr_l, tail_r, tail_l, tail_r_in, tail_l_in, mask_own, mask_prev,
+    load_sem, hs, hr, ss, sr, rs, rr, ms, mr,
+    os, orr, fs, fr, gs, gr, ds, dr, s2s, s2r, crs, crr, cls, clr,
 ):
     rows = x.shape[0]
     chunks = rows // KC
@@ -58,6 +62,8 @@
     last = n_ao - 1
     has_left = n > 0
     has_right = n < n_ao - 1
+    pair = a + 1 - 2 * lax.rem(a, 2)
+    mirror = AUX - 1 - a
     left = jnp.maximum(n - 1, 0)
     right = jnp.minimum(n + 1, n_ao - 1)
 
@@ -179,47 +185,84 @@
     def _():
         hal[:, :, BS:] = jnp.zeros((3, rows, BS), hal.dtype)
         tr_r[...] = jnp.zeros_like(tr_r)
+        tail_r_in[...] = jnp.zeros_like(tail_r_in)
         mask_prev[...] = jnp.zeros_like(mask_prev)
 
     @pl.when(jnp.logical_not(has_right))
     def _():
         hal[:, :, :BS] = jnp.zeros((3, rows, BS), hal.dtype)
         tr_l[...] = jnp.zeros_like(tr_l)
+        tail_l_in[...] = jnp.zeros_like(tail_l_in)
 
     acc[...] = jnp.zeros_like(acc)
 
-    def inner_step(c, carry):
-        load(c).wait()
-        piece = pl.ds(pl.multiple_of(c * KC, KC), KC)
-        for b in range(NBLK):
-            xt[c, b * BS:(b + 1) * BS, :] = x[piece, b * BS:(b + 1) * BS].T
-        for q in range(4):
-            lhs = xt[c, 0:INNER_M[q] * BS, :]
-            rhs = x[piece, 2 * q * BS:(2 * q + 2) * BS]
-            where = slice(INNER_OFF[q] * BS, (INNER_OFF[q] + INNER_M[q]) * BS)
-            acc[where, :] += jnp.dot(lhs, rhs, preferred_element_type=jnp.float32)
-        return carry
-
-    lax.fori_loop(0, chunks, inner_step, 0)
-    relay(0)
+    def inner_step(turned, wide, first):
+        def step(c, carry):
+            if first:
+                load(c).wait()
+            piece = pl.ds(pl.multiple_of(c * KC, KC), KC)
+            for b in turned:
+                xt[c, b * BS:(b + 1) * BS, :] = x[piece, b * BS:(b + 1) * BS].T
+            for q in wide:
+                lhs = xt[c, 0:INNER_M[q] * BS, :]
+                rhs = x[piece, 2 * q * BS:(2 * q + 2) * BS]
+                where = slice(INNER_OFF[q] * BS, (INNER_OFF[q] + INNER_M[q]) * BS)
+                acc[where, :] += jnp.dot(lhs, rhs, preferred_element_type=jnp.float32)
+            return carry
+
+        lax.fori_loop(0, chunks, step, 0)
+
+    def scaled(tile, keep):
+        return (tile * (keep > 0).astype(jnp.float32)).astype(part.dtype)
 
     def put(tile, keep, t):
-        scaled = tile * (keep > 0).astype(jnp.float32)
-        part[:, t] = scaled.astype(part.dtype).reshape(AUX, SL, BS)
-
-    for t, (i, j) in enumerate(INNER):
-        row = (INNER_OFF[j // 2] + i) * BS
-        col = (j % 2) * BS
-        put(acc[row:row + BS, col:col + BS], mask_own[i:i + 1, j - i - 1:j - i], t)
-
-    def send1(k, r):
-        span = pl.ds(T0[k], T0[k + 1] - T0[k])
-        return pltpu.make_async_remote_copy(
-            part.at[aux_peer(r), span], rbuf.at[r - 1, span],
-            s1s.at[k, r - 1], s1r.at[k, r - 1], device_id={"aux": aux_peer(r)}, device_id_type=MESH)
-
-    for r in range(1, AUX):
-        send1(0, r).start()
+        part[:, t] = scaled(tile, keep).reshape(AUX, SL, BS)
+
+    def put_inner(k):
+        for u, (i, j) in enumerate(INNER_PART[k]):
+            row = (INNER_OFF[j // 2] + i) * BS
+            col = (j % 2) * BS
+            put(acc[row:row + BS, col:col + BS], mask_own[i:i + 1, j - i - 1:j - i], T0[k] + u)
+
+    def span_of(k):
+        return pl.ds(T0[k], T0[k + 1] - T0[k])
+
+    def send_far(k):
+        return pltpu.make_async_remote_copy(
+            part.at[AUX - 1 - pair, span_of(k)], far_sum.at[span_of(k)],
+            fs.at[k], fr.at[k], device_id={"aux": pair}, device_id_type=MESH)
+
+    def send_own(k):
+        return pltpu.make_async_remote_copy(
+            part.at[pair, span_of(k)], own_sum.at[span_of(k)],
+            os.at[k], orr.at[k], device_id={"aux": pair}, device_id_type=MESH)
+
+    def send_mirror(k):
+        return pltpu.make_async_remote_copy(
+            far_out.at[span_of(k)], far_in.at[span_of(k)],
+            gs.at[k], gr.at[k], device_id={"aux": mirror}, device_id_type=MESH)
+
+    def alpha(k):
+        send_far(k).start()
+        send_own(k).start()
+
+    def beta(k):
+        send_far(k).wait_recv()
+        for t in range(T0[k], T0[k + 1]):
+            far_out[t] = (part[mirror, t].astype(jnp.float32) + far_sum[t].astype(jnp.float32)).astype(part.dtype)
+        send_mirror(k).start()
+
+    def send_tail(r):
+        return pltpu.make_async_remote_copy(
+            part.at[aux_peer(r), pl.ds(TAIL, N_ALL - TAIL)], tail_in.at[r - 1],
+            ds.at[r - 1], dr.at[r - 1], device_id={"aux": aux_peer(r)}, device_id_type=MESH)
+
+    inner_step(range(0, 5), range(0, 3), True)
+    put_inner(0)
+    alpha(0)
+    inner_step(range(5, NBLK), range(3, 4), False)
+    put_inner(1)
+    alpha(1)
 
     def cross(b):
         @pl.when(near_right)
@@ -250,25 +293,28 @@
             return carry
 
         lax.fori_loop(0, chunks, step, 0)
-        t = T0[b + 1]
-        for i, j in RIGHT[b]:
+        t = T0[b + 2]
+        for u, (i, j) in enumerate(RIGHT[b]):
             own = NBLK - 1 - i
             row = (own - LO[b]) * BS
-            put(acc[row:row + BS, 0:BS], mask_own[own:own + 1, i + j:i + j + 1], t)
+            tile = acc[row:row + BS, 0:BS]
+            keep = mask_own[own:own + 1, i + j:i + j + 1]
+            put(tile, keep, t)
+            if b == 2:
+                tail_r[:, u] = scaled(tile.T, keep).reshape(AUX, SL, BS)
             t += 1
-        for i, j in LEFT[b]:
+        for u, (i, j) in enumerate(LEFT[b]):
             row = (j - LO[b]) * BS
             far = NBLK - 1 - i
-            put(acc[row:row + BS, BS:2 * BS], mask_prev[far:far + 1, i + j:i + j + 1], t)
+            tile = acc[row:row + BS, BS:2 * BS]
+            keep = mask_prev[far:far + 1, i + j:i + j + 1]
+            put(tile, keep, t)
+            if b == 2:
+                tail_l[:, u] = scaled(tile.T, keep).reshape(AUX, SL, BS)
             t += 1
-        for r in range(1, AUX):
-            send1(b + 1, r).start()
 
     def total(t):
-        value = part[a, t].astype(jnp.float32)
-        for r in range(1, AUX):
-            value = value + rbuf[r - 1, t].astype(jnp.float32)
-        return value
+        return part[a, t].astype(jnp.float32) + own_sum[t].astype(jnp.float32) + far_in[t].astype(jnp.float32)
 
     def turn(values, ts, g):
         values = values + [jnp.zeros((SL, BS), jnp.float32)] * (4 - len(values))
@@ -283,9 +329,10 @@
                 values.append(value)
             turn(values, ts, g0 + g)
 
-    def send_in(r):
-        return pltpu.make_async_remote_copy(
-            ts_in.at[aux_peer(r)], tr_in.at[a], s2s.at[r - 1], s2r.at[r - 1],
+    def send_in(k, r):
+        span = pl.ds(GI[k], GI[k + 1] - GI[k])
+        return pltpu.make_async_remote_copy(
+            ts_in.at[aux_peer(r), span], tr_in.at[a, span], s2s.at[k, r - 1], s2r.at[k, r - 1],
             device_id={"aux": aux_peer(r)}, device_id_type=MESH)
 
     def send_r(b, to):
@@ -312,18 +359,18 @@
             ts_l.at[source, span], tr_l.at[source, span], cls.at[b, source], clr.at[b, source],
             device_id={"ao": right, "aux": source}, device_id_type=MESH)
 
-    def inner_sums():
+    def inner_sums(k):
+        send_own(k).wait_recv()
+        send_mirror(k).wait_recv()
+        sums(T0[k], [(i, W + j - i - 1) for i, j in INNER_PART[k]], ts_in, GI[k])
+        tr_in[a, GI[k]:GI[k + 1]] = ts_in[a, GI[k]:GI[k + 1]]
         for r in range(1, AUX):
-            send1(0, r).wait_recv()
-        sums(0, [(i, W + j - i - 1) for i, j in INNER], ts_in, 0)
-        tr_in[a] = ts_in[a]
-        for r in range(1, AUX):
-            send_in(r).start()
+            send_in(k, r).start()
 
     def cross_sums(b):
-        for r in range(1, AUX):
-            send1(b + 1, r).wait_recv()
-        t = T0[b + 1]
+        send_own(b + 2).wait_recv()
+        send_mirror(b + 2).wait_recv()
+        t = T0[b + 2]
         sums(t, [(NBLK - 1 - i, W + i + j) for i, j in RIGHT[b]], ts_r, GR[b])
 
         @pl.when(has_right)
@@ -344,10 +391,10 @@
             pieces = [tr[source, g, :, v * SL:(v + 1) * SL].astype(jnp.float32) for source in range(AUX)]
             out_ref[m, e] = jnp.concatenate(pieces, axis=1)
 
-    def inner_place():
+    def inner_place(k):
         for r in range(1, AUX):
-            send_in(r).wait_recv()
-        place(tr_in, 0, [(j, W - (j - i)) for i, j in INNER])
+            send_in(k, r).wait_recv()
+        place(tr_in, GI[k], [(j, W - (j - i)) for i, j in INNER_PART[k]])
 
     def cross_place(b):
         @pl.when(has_left)
@@ -364,37 +411,116 @@
 
         place(tr_l, GL[b], [(NBLK - 1 - i, W + i + j) for i, j in LEFT[b]])
 
+    def tail_to_right(to):
+        return pltpu.make_async_remote_copy(
+            tail_r.at[to], tail_r_in.at[a], crs.at[2, to], crr.at[2, a],
+            device_id={"ao": right, "aux": to}, device_id_type=MESH)
+
+    def tail_to_left(to):
+        return pltpu.make_async_remote_copy(
+            tail_l.at[to], tail_l_in.at[a], cls.at[2, to], clr.at[2, a],
+            device_id={"ao": left, "aux": to}, device_id_type=MESH)
+
+    def tail_from_left(source):
+        return pltpu.make_async_remote_copy(
+            tail_r.at[source], tail_r_in.at[source], crs.at[2, source], crr.at[2, source],
+            device_id={"ao": left, "aux": source}, device_id_type=MESH)
+
+    def tail_from_right(source):
+        return pltpu.make_async_remote_copy(
+            tail_l.at[source], tail_l_in.at[source], cls.at[2, source], clr.at[2, source],
+            device_id={"ao": right, "aux": source}, device_id_type=MESH)
+
+    def tail_send():
+        for r in range(1, AUX):
+            send_tail(r).start()
+
+        @pl.when(has_right)
+        def _():
+            for to in range(AUX):
+                tail_to_right(to).start()
+
+        @pl.when(has_left)
+        def _():
+            for to in range(AUX):
+                tail_to_left(to).start()
+
+    def tail_finish():
+        for r in range(1, AUX):
+            send_tail(r).wait_recv()
+        places = [(NBLK - 1 - i, W + i + j) for i, j in RIGHT[2]] + [(j, W - 1 - i - j) for i, j in LEFT[2]]
+        for u, (m, e) in enumerate(places):
+            value = part[a, TAIL + u].astype(jnp.float32)
+            for r in range(1, AUX):
+                value = value + tail_in[r - 1, u].astype(jnp.float32)
+            out_ref[m, e] = value
+
+        @pl.when(has_left)
+        def _():
+            for source in range(AUX):
+                tail_from_left(source).wait_recv()
+
+        @pl.when(has_right)
+        def _():
+            for source in range(AUX):
+                tail_from_right(source).wait_recv()
+
+        for u, (i, j) in enumerate(RIGHT[2]):
+            value = tail_r_in[0, u].astype(jnp.float32)
+            for source in range(1, AUX):
+                value = value + tail_r_in[source, u].astype(jnp.float32)
+            out_ref[j, W - 1 - i - j] = value
+        for u, (i, j) in enumerate(LEFT[2]):
+            value = tail_l_in[0, u].astype(jnp.float32)
+            for source in range(1, AUX):
+                value = value + tail_l_in[source, u].astype(jnp.float32)
+            out_ref[NBLK - 1 - i, W + i + j] = value
+
+    relay(0)
+    beta(0)
     relay(1)
     cross(0)
+    alpha(2)
     relay(2)
+    beta(1)
+    beta(2)
+    inner_sums(0)
+    inner_sums(1)
     cross(1)
-    inner_sums()
+    alpha(3)
     cross_sums(0)
+    inner_place(0)
+    inner_place(1)
+    beta(3)
     cross(2)
+    tail_send()
     cross_sums(1)
-    inner_place()
     cross_place(0)
-    cross_sums(2)
     cross_place(1)
-    cross_place(2)
+    tail_finish()
 
     for k in range(4):
-        for r in range(1, AUX):
-            send1(k, r).wait_send()
+        send_far(k).wait_send()
+        send_own(k).wait_send()
+        send_mirror(k).wait_send()
     for r in range(1, AUX):
-        send_in(r).wait_send()
+        send_tail(r).wait_send()
+        for k in range(2):
+            send_in(k, r).wait_send()
 
     @pl.when(has_right)
     def _():
         mask_copy.wait_send()
-        for b in range(3):
-            for to in range(AUX):
+        for to in range(AUX):
+            tail_to_right(to).wait_send()
+            for b in range(2):
                 send_r(b, to).wait_send()
 
     @pl.when(has_left)
     def _():
-        for b in range(3):
-            for to in range(AUX):
+        for to in range(AUX):
+            tail_to_left(to).wait_send()
+            for b in range(2):
                 send_l(b, to).wait_send()
 
     for b in range(3):
@@ -434,21 +560,32 @@
             pltpu.VMEM((3, rows // AUX, BS), bf16),
             pltpu.VMEM((sum(INNER_M) * BS, 2 * BS), jnp.float32),
             pltpu.VMEM((AUX, N_ALL, SL, BS), bf16),
-            pltpu.VMEM((AUX - 1, N_ALL, SL, BS), bf16),
-            pltpu.VMEM((AUX, G_IN, SL, BS), bf16),
-            pltpu.VMEM((AUX, GR[3], SL, BS), bf16),
-            pltpu.VMEM((AUX, GL[3], SL, BS), bf16),
-            pltpu.VMEM((AUX, G_IN, SL, BS), bf16),
-            pltpu.VMEM((AUX, GR[3], SL, BS), bf16),
-            pltpu.VMEM((AUX, GL[3], SL, BS), bf16),
+            pltpu.VMEM((TAIL, SL, BS), bf16),
+            pltpu.VMEM((TAIL, SL, BS), bf16),
+            pltpu.VMEM((TAIL, SL, BS), bf16),
+            pltpu.VMEM((TAIL, SL, BS), bf16),
+            pltpu.VMEM((AUX - 1, N_ALL - TAIL, SL, BS), bf16),
+            pltpu.VMEM((AUX, GI[2], SL, BS), bf16),
+            pltpu.VMEM((AUX, GR[2], SL, BS), bf16),
+            pltpu.VMEM((AUX, GL[2], SL, BS), bf16),
+            pltpu.VMEM((AUX, GI[2], SL, BS), bf16),
+            pltpu.VMEM((AUX, GR[2], SL, BS), bf16),
+            pltpu.VMEM((AUX, GL[2], SL, BS), bf16),
+            pltpu.VMEM((AUX, len(RIGHT[2]), SL, BS), bf16),
+            pltpu.VMEM((AUX, len(LEFT[2]), SL, BS), bf16),
+            pltpu.VMEM((AUX, len(RIGHT[2]), SL, BS), bf16),
+            pltpu.VMEM((AUX, len(LEFT[2]), SL, BS), bf16),
             pltpu.VMEM((NBLK, BS), jnp.int32),
             pltpu.VMEM((NBLK, BS), jnp.int32),
             dma((rows // KC,)),
             dma((2, 3)), dma((2, 3)),
             dma((AUX, 3)), dma((AUX, 3)), dma((3,)), dma((3,)),
             dma, dma,
-            dma((4, AUX - 1)), dma((4, AUX - 1)),
+            dma((4,)), dma((4,)),
+            dma((4,)), dma((4,)),
+            dma((4,)), dma((4,)),
             dma((AUX - 1,)), dma((AUX - 1,)),
+            dma((2, AUX - 1)), dma((2, AUX - 1)),
             dma((3, AUX)), dma((3, AUX)),
             dma((3, AUX)), dma((3, AUX)),
         ],

time: 81.4 us -> 72.9 us (0.90)
  Pallas kernels: 78.8 us -> 71 us
    pallas_call x1, Pallas kernels: 78.8 us -> 71 us  [body(): pl.pallas_call(kernel, out_shape=jax.ShapeDtypeStruct((NBLK, 2 * W, SL, B...]
where the time goes in v3:
time: 72.9 us; the launch traced here: 72.8 us
  Pallas kernels  71 us (97%)
  local copies, waits for them, and re-layouts  1.83 us (3%)
    pallas_call x1, Pallas kernels, body(): pl.pallas_call(kernel, out_shape=jax.ShapeDtypeStruct((NBLK, 2 * W, SL, B...  71 us
    unnamed x3, local copies, waits for them, and re-layouts  1.83 us

profile of v3, /device:TPU:31, one launch (start us, length us, event | category | flops | bytes accessed | tf_op | source)
XLA Modules:
  0.0 72.8 jit_solution(62269437984873822)
XLA Ops:
  0.0 0.0 copy-start
  0.0 0.7 copy-done
  0.7 71.0 %shard_map.28 = f32[8,12,32,128]{3,2,1,0:T(8,128)S(1)} custom-call(bf16[4096,1024]{1,0:T(8,128)(2,1)} %bitcast.1, s32[8,6]{1,0:T(8,128)S(1)} %copy-done), custom_call_target="tpu_custom_call" | custom-call | flops 8589934592 | bytes 16777216 | tf_op jit(solution)/shard_map/pallas_call | solution.py:551
  71.7 1.1 %copy.4 = f32[8,12,32,128]{3,2,1,0:T(8,128)} copy(f32[8,12,32,128]{3,2,1,0:T(8,128)S(1)} %shard_map.28) | data formatting | bytes 3145728
Async XLA Ops:
  0.0 0.7 copy-start

commit v4 on v3

--- a/solution.py
+++ b/solution.py
@@ -15,7 +15,9 @@
 SL = BS // AUX
 KC = 1024
 SEAM = 31
-RELAY = [7, 15, 0]
+RELAY = [7, 15, 23, 0]
+CUTS = [0, 512, 1536, 2560, 3584, 4096]
+PATHS = len(RELAY) + 1
 
 INNER = [(i, j) for j in range(1, NBLK) for i in range(max(0, j - W), j)]
 INNER_M = [1, 3, 5, 7]
@@ -63,7 +65,8 @@
     has_left = n > 0
     has_right = n < n_ao - 1
     pair = a + 1 - 2 * lax.rem(a, 2)
-    mirror = AUX - 1 - a
+    outer = (a == 0) | (a == AUX - 1)
+    other_half = jnp.where(a < 2, 2, 0)
     left = jnp.maximum(n - 1, 0)
     right = jnp.minimum(n + 1, n_ao - 1)
 
@@ -84,8 +87,6 @@
         for b in range(AUX):
             pl.semaphore_signal(barrier, 1, device_id={"ao": right, "aux": b}, device_id_type=MESH)
 
-    quarter = rows // AUX
-
     def relay_of(p):
         return jnp.where(fwd, RELAY[p - 1], last - RELAY[p - 1])
 
@@ -94,8 +95,8 @@
 
     relay_to = jnp.where(fwd, SEAM + 1, SEAM)
     relay_from = jnp.where(fwd, SEAM, SEAM + 1)
-    extra = jnp.where(at_seam, AUX - 1, 0)
-    for p in range(1, AUX):
+    extra = jnp.where(at_seam, PATHS - 1, 0)
+    for p in range(1, PATHS):
         extra += jnp.where(is_relay(p), 1, 0)
 
         @pl.when(is_relay(p))
@@ -130,7 +131,10 @@
             hs.at[1, b], hr.at[1, b], device_id={"ao": right}, device_id_type=MESH)
 
     def seam_span(p, lanes):
-        return (pl.ds(p * quarter, quarter), pl.ds(pl.multiple_of(lanes, BS), BS))
+        return (pl.ds(CUTS[p], CUTS[p + 1] - CUTS[p]), pl.ds(pl.multiple_of(lanes, BS), BS))
+
+    def parked(b, p):
+        return rel.at[b, pl.ds(0, CUTS[p + 1] - CUTS[p])]
 
     def seam_out(b, p):
         source = x_hbm.at[seam_span(p, jnp.where(fwd, (NBLK - 1 - b) * BS, b * BS))]
@@ -139,20 +143,20 @@
                 source, hal.at[(b,) + seam_span(p, jnp.where(fwd, BS, 0))],
                 ss.at[p, b], sr.at[p, b], device_id={"ao": relay_to}, device_id_type=MESH)
         return pltpu.make_async_remote_copy(
-            source, rel.at[b], ss.at[p, b], rr.at[b], device_id={"ao": relay_of(p)}, device_id_type=MESH)
+            source, parked(b, p), ss.at[p, b], rr.at[b], device_id={"ao": relay_of(p)}, device_id_type=MESH)
 
     def relay_out(b, p):
         return pltpu.make_async_remote_copy(
-            rel.at[b], hal.at[(b,) + seam_span(p, jnp.where(fwd, BS, 0))],
+            parked(b, p), hal.at[(b,) + seam_span(p, jnp.where(fwd, BS, 0))],
             rs.at[b], sr.at[p, b], device_id={"ao": relay_to}, device_id_type=MESH)
 
     def seam_in(b, p):
         return pltpu.make_async_remote_copy(
-            rel.at[b], hal.at[(b,) + seam_span(p, jnp.where(fwd, 0, BS))],
+            parked(b, p), hal.at[(b,) + seam_span(p, jnp.where(fwd, 0, BS))],
             rs.at[b], sr.at[p, b], device_id={"ao": relay_to}, device_id_type=MESH)
 
     def relay(b):
-        for p in range(1, AUX):
+        for p in range(1, PATHS):
             @pl.when(is_relay(p))
             def _():
                 seam_out(b, p).wait_recv()
@@ -178,7 +182,7 @@
 
         @pl.when(at_seam)
         def _():
-            for p in (1, 3, 2, 0):
+            for p in (1, 2, 4, 3, 0):
                 seam_out(b, p).start()
 
     @pl.when(jnp.logical_not(has_left))
@@ -229,7 +233,7 @@
 
     def send_far(k):
         return pltpu.make_async_remote_copy(
-            part.at[AUX - 1 - pair, span_of(k)], far_sum.at[span_of(k)],
+            part.at[pl.ds(other_half, 2), span_of(k)], far_sum.at[:, span_of(k)],
             fs.at[k], fr.at[k], device_id={"aux": pair}, device_id_type=MESH)
 
     def send_own(k):
@@ -237,20 +241,28 @@
             part.at[pair, span_of(k)], own_sum.at[span_of(k)],
             os.at[k], orr.at[k], device_id={"aux": pair}, device_id_type=MESH)
 
-    def send_mirror(k):
-        return pltpu.make_async_remote_copy(
-            far_out.at[span_of(k)], far_in.at[span_of(k)],
-            gs.at[k], gr.at[k], device_id={"aux": mirror}, device_id_type=MESH)
+    def send_joined(k, h):
+        return pltpu.make_async_remote_copy(
+            far_out.at[h, span_of(k)], far_in.at[span_of(k)],
+            gs.at[k, h], gr.at[k], device_id={"aux": other_half + h}, device_id_type=MESH)
 
     def alpha(k):
-        send_far(k).start()
+        @pl.when(outer)
+        def _():
+            send_far(k).start()
+
         send_own(k).start()
 
     def beta(k):
-        send_far(k).wait_recv()
-        for t in range(T0[k], T0[k + 1]):
-            far_out[t] = (part[mirror, t].astype(jnp.float32) + far_sum[t].astype(jnp.float32)).astype(part.dtype)
-        send_mirror(k).start()
+        @pl.when(jnp.logical_not(outer))
+        def _():
+            send_far(k).wait_recv()
+            for h in range(2):
+                for t in range(T0[k], T0[k + 1]):
+                    far_out[h, t] = (
+                        part[other_half + h, t].astype(jnp.float32) + far_sum[h, t].astype(jnp.float32)
+                    ).astype(part.dtype)
+                send_joined(k, h).start()
 
     def send_tail(r):
         return pltpu.make_async_remote_copy(
@@ -260,6 +272,7 @@
     inner_step(range(0, 5), range(0, 3), True)
     put_inner(0)
     alpha(0)
+    relay(0)
     inner_step(range(5, NBLK), range(3, 4), False)
     put_inner(1)
     alpha(1)
@@ -275,7 +288,7 @@
 
         @pl.when(at_seam)
         def _():
-            for p in range(AUX):
+            for p in range(PATHS):
                 seam_in(b, p).wait_recv()
 
         if b == 0:
@@ -361,7 +374,7 @@
 
     def inner_sums(k):
         send_own(k).wait_recv()
-        send_mirror(k).wait_recv()
+        send_joined(k, 0).wait_recv()
         sums(T0[k], [(i, W + j - i - 1) for i, j in INNER_PART[k]], ts_in, GI[k])
         tr_in[a, GI[k]:GI[k + 1]] = ts_in[a, GI[k]:GI[k + 1]]
         for r in range(1, AUX):
@@ -369,7 +382,7 @@
 
     def cross_sums(b):
         send_own(b + 2).wait_recv()
-        send_mirror(b + 2).wait_recv()
+        send_joined(b + 2, 0).wait_recv()
         t = T0[b + 2]
         sums(t, [(NBLK - 1 - i, W + i + j) for i, j in RIGHT[b]], ts_r, GR[b])
 
@@ -476,7 +489,6 @@
                 value = value + tail_l_in[source, u].astype(jnp.float32)
             out_ref[NBLK - 1 - i, W + i + j] = value
 
-    relay(0)
     beta(0)
     relay(1)
     cross(0)
@@ -500,9 +512,17 @@
     tail_finish()
 
     for k in range(4):
-        send_far(k).wait_send()
         send_own(k).wait_send()
-        send_mirror(k).wait_send()
+
+        @pl.when(outer)
+        def _():
+            send_far(k).wait_send()
+
+        @pl.when(jnp.logical_not(outer))
+        def _():
+            for h in range(2):
+                send_joined(k, h).wait_send()
+
     for r in range(1, AUX):
         send_tail(r).wait_send()
         for k in range(2):
@@ -534,10 +554,10 @@
 
         @pl.when(at_seam)
         def _():
-            for p in range(AUX):
+            for p in range(PATHS):
                 seam_out(b, p).wait_send()
 
-        for p in range(1, AUX):
+        for p in range(1, PATHS):
             @pl.when(is_relay(p))
             def _():
                 relay_out(b, p).wait_send()
@@ -557,12 +577,12 @@
             pltpu.VMEM((rows, NBLK * BS), bf16),
             pltpu.VMEM((rows // KC, NBLK * BS, KC), bf16),
             pltpu.VMEM((3, rows, 2 * BS), bf16),
-            pltpu.VMEM((3, rows // AUX, BS), bf16),
+            pltpu.VMEM((3, max(CUTS[p + 1] - CUTS[p] for p in range(1, PATHS)), BS), bf16),
             pltpu.VMEM((sum(INNER_M) * BS, 2 * BS), jnp.float32),
             pltpu.VMEM((AUX, N_ALL, SL, BS), bf16),
             pltpu.VMEM((TAIL, SL, BS), bf16),
-            pltpu.VMEM((TAIL, SL, BS), bf16),
-            pltpu.VMEM((TAIL, SL, BS), bf16),
+            pltpu.VMEM((2, TAIL, SL, BS), bf16),
+            pltpu.VMEM((2, TAIL, SL, BS), bf16),
             pltpu.VMEM((TAIL, SL, BS), bf16),
             pltpu.VMEM((AUX - 1, N_ALL - TAIL, SL, BS), bf16),
             pltpu.VMEM((AUX, GI[2], SL, BS), bf16),
@@ -579,11 +599,11 @@
             pltpu.VMEM((NBLK, BS), jnp.int32),
             dma((rows // KC,)),
             dma((2, 3)), dma((2, 3)),
-            dma((AUX, 3)), dma((AUX, 3)), dma((3,)), dma((3,)),
+            dma((PATHS, 3)), dma((PATHS, 3)), dma((3,)), dma((3,)),
             dma, dma,
             dma((4,)), dma((4,)),
             dma((4,)), dma((4,)),
-            dma((4,)), dma((4,)),
+            dma((4, 2)), dma((4,)),
             dma((AUX - 1,)), dma((AUX - 1,)),
             dma((2, AUX - 1)), dma((2, AUX - 1)),
             dma((3, AUX)), dma((3, AUX)),

time: 72.9 us -> 67 us (0.919)
  Pallas kernels: 71 us -> 64.7 us
    pallas_call x1, Pallas kernels: 71 us -> 64.7 us  [body(): pl.pallas_call(kernel, out_shape=jax.ShapeDtypeStruct((NBLK, 2 * W, SL, B...]
where the time goes in v4:
time: 67 us; the launch traced here: 66.5 us
  Pallas kernels  64.7 us (97%)
  local copies, waits for them, and re-layouts  1.83 us (3%)
    pallas_call x1, Pallas kernels, body(): pl.pallas_call(kernel, out_shape=jax.ShapeDtypeStruct((NBLK, 2 * W, SL, B...  64.7 us
    unnamed x3, local copies, waits for them, and re-layouts  1.83 us

profile of v4, /device:TPU:31, one launch (start us, length us, event | category | flops | bytes accessed | tf_op | source)
XLA Modules:
  0.0 66.5 jit_solution(5220425308225094125)
XLA Ops:
  0.0 0.0 copy-start
  0.0 0.7 %copy-done = s32[8,6]{1,0:T(8,128)S(1)} copy-done((s32[8,6]{1,0:T(8,128)S(1)}, s32[8,6]{1,0:T(8,128)}, u32[]{:S(2)}) %copy-start) | copy-done | bytes 216
  0.7 64.7 %shard_map.28 = f32[8,12,32,128]{3,2,1,0:T(8,128)S(1)} custom-call(bf16[4096,1024]{1,0:T(8,128)(2,1)} %bitcast.1, s32[8,6]{1,0:T(8,128)S(1)} %copy-done), custom_call_target="tpu_custom_call" | custom-call | flops 8589934592 | bytes 16777216 | tf_op jit(solution)/shard_map/pallas_call | solution.py:571
  65.3 1.1 %copy.4 = f32[8,12,32,128]{3,2,1,0:T(8,128)} copy(f32[8,12,32,128]{3,2,1,0:T(8,128)S(1)} %shard_map.28) | data formatting | bytes 3145728
Async XLA Ops:
  0.0 0.7 %copy-start = (s32[8,6]{1,0:T(8,128)S(1)}, s32[8,6]{1,0:T(8,128)}, u32[]{:S(2)}) copy-start(s32[8,6]{1,0:T(8,128)} %mask_ref.1) | copy-start | bytes 580

commit v5 on v4

v5 whole, which is shorter than its diff:
```python
import functools

import jax
import jax.numpy as jnp
from jax import lax
from jax.experimental import pallas as pl
from jax.experimental.pallas import tpu as pltpu
from jax.sharding import PartitionSpec as P

MESH = pl.DeviceIdType.MESH
BS = 128
W = 6
NBLK = 8
AUX = 4
SL = BS // AUX
KC = 1024
SEAM = 31
RELAY = [6, 14, 22, 0]
CUTS = [0, 640, 1536, 2560, 3456, 4096]
PATHS = len(RELAY) + 1

INNER = [(i, j) for j in range(1, NBLK) for i in range(max(0, j - W), j)]
INNER_M = [1, 3, 5, 7]
INNER_OFF = [0, 1, 4, 9]
RIGHT = [[(i, b) for i in range(b, W - b)] for b in range(3)]
LEFT = [[(b, j) for j in range(b + 1, W - b)] for b in range(3)]
def groups_of(count):
    return (count + 3) // 4


EARLY = 15
INNER_PART = [INNER[:EARLY], INNER[EARLY:]]
FAST, SLOW0, SLOW1, LAST = 2, 3, 4, 5
GI = [0, groups_of(EARLY), groups_of(EARLY) + groups_of(len(INNER) - EARLY)]
SIDES = {"R": RIGHT, "L": LEFT}
BASE = {"R": len(INNER), "L": len(INNER) + sum(map(len, RIGHT))}
N_ALL = BASE["L"] + sum(map(len, LEFT))
GX = {FAST: (0, 3), SLOW0: (0, 2), SLOW1: (2, 3)}


def tiles_of(k, side):
    if k < FAST:
        return INNER_PART[k]
    if k == FAST:
        return sum(SIDES[side], [])
    return SIDES[side][k - SLOW0]


def start_of(k, side):
    if k < FAST:
        return k * EARLY
    if k == FAST:
        return BASE[side]
    return BASE[side] + sum(map(len, SIDES[side][:k - SLOW0]))


def rows_of(side, b):
    return (2 + b, NBLK - b) if side == "R" else (1 + b, W - b)


def kernel(
    x_hbm, mask_hbm, out_ref,
    x, xt, hal, rel, acc, part, own_sum, far_sum, far_out, far_in, tail_in,
    ts_in, ts_r, ts_l, tr_in, tr_r, tr_l, tail_r, tail_l, tail_r_in, tail_l_in, mask_own, mask_prev,
    load_sem, mask_sem, hs, hr, ss, sr, rs, rr, ms, mr,
    os, orr, fs, fr, gs, gr, ds, dr, s2s, s2r, cs, cr,
):
    rows = x.shape[0]
    chunks = rows // KC
    n = lax.axis_index("ao")
    a = lax.axis_index("aux")
    n_ao = lax.axis_size("ao")
    fwd = n <= SEAM
    at_seam = (n == SEAM) | (n == SEAM + 1)
    last = n_ao - 1
    even = lax.rem(n, 2) == 0
    has_left = n > 0
    has_right = n < n_ao - 1
    pair = a + 1 - 2 * lax.rem(a, 2)
    outer = (a == 0) | (a == AUX - 1)
    other_half = jnp.where(a < 2, 2, 0)
    left = jnp.maximum(n - 1, 0)
    right = jnp.minimum(n + 1, n_ao - 1)

    def aux_peer(r):
        return lax.rem(a + r, AUX)

    barrier = pltpu.get_barrier_semaphore()
    for r in range(1, AUX):
        pl.semaphore_signal(barrier, 1, device_id={"aux": aux_peer(r)}, device_id_type=MESH)

    @pl.when(has_left)
    def _():
        for b in range(AUX):
            pl.semaphore_signal(barrier, 1, device_id={"ao": left, "aux": b}, device_id_type=MESH)

    @pl.when(has_right)
    def _():
        for b in range(AUX):
            pl.semaphore_signal(barrier, 1, device_id={"ao": right, "aux": b}, device_id_type=MESH)

    def relay_of(p):
        return jnp.where(fwd, RELAY[p - 1], last - RELAY[p - 1])

    def is_relay(p):
        return n == relay_of(p)

    relay_to = jnp.where(fwd, SEAM + 1, SEAM)
    relay_from = jnp.where(fwd, SEAM, SEAM + 1)
    extra = jnp.where(at_seam, PATHS - 1, 0)
    for p in range(1, PATHS):
        extra += jnp.where(is_relay(p), 1, 0)

        @pl.when(is_relay(p))
        def _():
            pl.semaphore_signal(barrier, 1, device_id={"ao": relay_from}, device_id_type=MESH)

        @pl.when(at_seam)
        def _():
            other = jnp.where(fwd, last - RELAY[p - 1], RELAY[p - 1])
            pl.semaphore_signal(barrier, 1, device_id={"ao": other}, device_id_type=MESH)

    def load(c):
        piece = pl.ds(pl.multiple_of(c * KC, KC), KC)
        return pltpu.make_async_copy(x_hbm.at[piece], x.at[piece], load_sem.at[c])

    for c in range(chunks):
        load(c).start()
    mask_load = pltpu.make_async_copy(mask_hbm, mask_own, mask_sem)
    mask_load.start()

    pl.semaphore_wait(
        barrier, AUX - 1 + AUX * (has_left.astype(jnp.int32) + has_right.astype(jnp.int32)) + extra)

    def to_left(b):
        return pltpu.make_async_remote_copy(
            x_hbm.at[:, pl.ds(b * BS, BS)], hal.at[b, :, pl.ds(0, BS)],
            hs.at[0, b], hr.at[0, b], device_id={"ao": left}, device_id_type=MESH)

    def to_right(b):
        return pltpu.make_async_remote_copy(
            x_hbm.at[:, pl.ds((NBLK - 1 - b) * BS, BS)], hal.at[b, :, pl.ds(BS, BS)],
            hs.at[1, b], hr.at[1, b], device_id={"ao": right}, device_id_type=MESH)

    def seam_span(p, lanes):
        return (pl.ds(CUTS[p], CUTS[p + 1] - CUTS[p]), pl.ds(pl.multiple_of(lanes, BS), BS))

    def parked(b, p):
        return rel.at[b, pl.ds(0, CUTS[p + 1] - CUTS[p])]

    def seam_out(b, p):
        source = x_hbm.at[seam_span(p, jnp.where(fwd, (NBLK - 1 - b) * BS, b * BS))]
        if p == 0:
            return pltpu.make_async_remote_copy(
                source, hal.at[(b,) + seam_span(p, jnp.where(fwd, BS, 0))],
                ss.at[p, b], sr.at[p, b], device_id={"ao": relay_to}, device_id_type=MESH)
        return pltpu.make_async_remote_copy(
            source, parked(b, p), ss.at[p, b], rr.at[b], device_id={"ao": relay_of(p)}, device_id_type=MESH)

    def relay_out(b, p):
        return pltpu.make_async_remote_copy(
            parked(b, p), hal.at[(b,) + seam_span(p, jnp.where(fwd, BS, 0))],
            rs.at[b], sr.at[p, b], device_id={"ao": relay_to}, device_id_type=MESH)

    def seam_in(b, p):
        return pltpu.make_async_remote_copy(
            parked(b, p), hal.at[(b,) + seam_span(p, jnp.where(fwd, 0, BS))],
            rs.at[b], sr.at[p, b], device_id={"ao": relay_to}, device_id_type=MESH)

    def relay(b):
        for p in range(1, PATHS):
            @pl.when(is_relay(p))
            def _():
                seam_out(b, p).wait_recv()
                relay_out(b, p).start()

    near_left = has_left & (n != SEAM + 1)
    near_right = has_right & (n != SEAM)
    mask_copy = pltpu.make_async_remote_copy(
        mask_own, mask_prev, ms, mr, device_id={"ao": right}, device_id_type=MESH)

    mask_load.wait()

    @pl.when(has_right)
    def _():
        mask_copy.start()

    for b in range(3):
        @pl.when(near_left)
        def _():
            to_left(b).start()

        @pl.when(near_right)
        def _():
            to_right(b).start()

        @pl.when(at_seam)
        def _():
            for p in (1, 2, 4, 3, 0):
                seam_out(b, p).start()

    @pl.when(jnp.logical_not(has_left))
    def _():
        hal[:, :, BS:] = jnp.zeros((3, rows, BS), hal.dtype)
        tr_r[...] = jnp.zeros_like(tr_r)
        tail_r_in[...] = jnp.zeros_like(tail_r_in)
        mask_prev[...] = jnp.zeros_like(mask_prev)

    @pl.when(jnp.logical_not(has_right))
    def _():
        hal[:, :, :BS] = jnp.zeros((3, rows, BS), hal.dtype)
        tr_l[...] = jnp.zeros_like(tr_l)
        tail_l_in[...] = jnp.zeros_like(tail_l_in)

    acc[...] = jnp.zeros_like(acc)

    def inner_step(turned, wide, first):
        def step(c, carry):
            if first:
                load(c).wait()
            piece = pl.ds(pl.multiple_of(c * KC, KC), KC)
            for b in turned:
                xt[c, b * BS:(b + 1) * BS, :] = x[piece, b * BS:(b + 1) * BS].T
            for q in wide:
                lhs = xt[c, 0:INNER_M[q] * BS, :]
                rhs = x[piece, 2 * q * BS:(2 * q + 2) * BS]
                where = slice(INNER_OFF[q] * BS, (INNER_OFF[q] + INNER_M[q]) * BS)
                acc[where, :] += jnp.dot(lhs, rhs, preferred_element_type=jnp.float32)
            return carry

        lax.fori_loop(0, chunks, step, 0)

    def scaled(tile, keep):
        return (tile * (keep > 0).astype(jnp.float32)).astype(part.dtype)

    def put(tile, keep, t):
        part[:, t] = scaled(tile, keep).reshape(AUX, SL, BS)

    def put_inner(k):
        for u, (i, j) in enumerate(INNER_PART[k]):
            row = (INNER_OFF[j // 2] + i) * BS
            col = (j % 2) * BS
            put(acc[row:row + BS, col:col + BS], mask_own[i:i + 1, j - i - 1:j - i], k * EARLY + u)

    def span_of(k, side):
        return pl.ds(start_of(k, side), len(tiles_of(k, side)))

    def send_far(k, side):
        return pltpu.make_async_remote_copy(
            part.at[pl.ds(other_half, 2), span_of(k, side)], far_sum.at[:, span_of(k, side)],
            fs.at[k], fr.at[k], device_id={"aux": pair}, device_id_type=MESH)

    def send_own(k, side):
        return pltpu.make_async_remote_copy(
            part.at[pair, span_of(k, side)], own_sum.at[span_of(k, side)],
            os.at[k], orr.at[k], device_id={"aux": pair}, device_id_type=MESH)

    def send_joined(k, h, side):
        return pltpu.make_async_remote_copy(
            far_out.at[h, span_of(k, side)], far_in.at[span_of(k, side)],
            gs.at[k, h], gr.at[k], device_id={"aux": other_half + h}, device_id_type=MESH)

    def alpha(k, side):
        @pl.when(outer)
        def _():
            send_far(k, side).start()

        send_own(k, side).start()

    def beta(k, side):
        @pl.when(jnp.logical_not(outer))
        def _():
            send_far(k, side).wait_recv()
            for h in range(2):
                for t in range(start_of(k, side), start_of(k, side) + len(tiles_of(k, side))):
                    far_out[h, t] = (
                        part[other_half + h, t].astype(jnp.float32) + far_sum[h, t].astype(jnp.float32)
                    ).astype(part.dtype)
                send_joined(k, h, side).start()

    def send_tail(r, side):
        count = len(tiles_of(LAST, side))
        return pltpu.make_async_remote_copy(
            part.at[aux_peer(r), span_of(LAST, side)], tail_in.at[r - 1, pl.ds(0, count)],
            ds.at[r - 1], dr.at[r - 1], device_id={"aux": aux_peer(r)}, device_id_type=MESH)

    inner_step(range(0, 5), range(0, 3), True)
    put_inner(0)
    alpha(0, None)
    relay(0)
    inner_step(range(5, NBLK), range(3, 4), False)
    put_inner(1)
    alpha(1, None)

    def arrive(side, b):
        if side == "R":
            @pl.when(near_right)
            def _():
                to_left(b).wait_recv()
        else:
            @pl.when(near_left)
            def _():
                to_right(b).wait_recv()

            if b == 0:
                @pl.when(has_left)
                def _():
                    mask_copy.wait_recv()

    def cross(side, b, slow):
        arrive(side, b)
        if slow:
            @pl.when(at_seam)
            def _():
                for p in range(PATHS):
                    seam_in(b, p).wait_recv()

        lo, hi = rows_of(side, b)
        size = (hi - lo) * BS
        lanes = slice(0, BS) if side == "R" else slice(BS, 2 * BS)
        acc[0:size, 0:BS] = jnp.zeros((size, BS), jnp.float32)

        def step(c, carry):
            piece = pl.ds(pl.multiple_of(c * KC, KC), KC)
            acc[0:size, 0:BS] += jnp.dot(
                xt[c, lo * BS:hi * BS, :], hal[b, piece, lanes], preferred_element_type=jnp.float32)
            return carry

        lax.fori_loop(0, chunks, step, 0)
        t0 = start_of(SLOW0 + b, side)
        for u, (i, j) in enumerate(SIDES[side][b]):
            far = NBLK - 1 - i
            row = ((far if side == "R" else j) - lo) * BS
            tile = acc[row:row + BS, 0:BS]
            keep = (mask_own if side == "R" else mask_prev)[far:far + 1, i + j:i + j + 1]
            put(tile, keep, t0 + u)
            if slow and b == 2:
                (tail_r if side == "R" else tail_l)[:, u] = scaled(tile.T, keep).reshape(AUX, SL, BS)

    def total(t):
        return part[a, t].astype(jnp.float32) + own_sum[t].astype(jnp.float32) + far_in[t].astype(jnp.float32)

    def turn(values, ts, g):
        values = values + [jnp.zeros((SL, BS), jnp.float32)] * (4 - len(values))
        ts[:, g] = jnp.concatenate(values, axis=0).T.astype(ts.dtype).reshape(AUX, SL, BS)

    def sums(t0, places, ts, g0):
        for g in range(groups_of(len(places))):
            values = []
            for u, (m, e) in enumerate(places[4 * g:4 * g + 4]):
                value = total(t0 + 4 * g + u)
                out_ref[m, e] = value
                values.append(value)
            turn(values, ts, g0 + g)

    def send_in(k, r):
        span = pl.ds(GI[k], GI[k + 1] - GI[k])
        return pltpu.make_async_remote_copy(
            ts_in.at[aux_peer(r), span], tr_in.at[a, span], s2s.at[k, r - 1], s2r.at[k, r - 1],
            device_id={"aux": aux_peer(r)}, device_id_type=MESH)

    def edge(side):
        return (has_right, right) if side == "R" else (has_left, left)

    def send_x(k, side, to):
        lo, hi = GX[k]
        ts, tr = (ts_r, tr_r) if side == "R" else (ts_l, tr_l)
        return pltpu.make_async_remote_copy(
            ts.at[to, pl.ds(lo, hi - lo)], tr.at[a, pl.ds(lo, hi - lo)], cs.at[k - FAST, to], cr.at[k - FAST, a],
            device_id={"ao": edge(side)[1], "aux": to}, device_id_type=MESH)

    def got_x(k, side, source):
        lo, hi = GX[k]
        ts, tr = (ts_r, tr_r) if side == "R" else (ts_l, tr_l)
        return pltpu.make_async_remote_copy(
            ts.at[source, pl.ds(lo, hi - lo)], tr.at[source, pl.ds(lo, hi - lo)],
            cs.at[k - FAST, source], cr.at[k - FAST, source],
            device_id={"ao": edge("L" if side == "R" else "R")[1], "aux": source}, device_id_type=MESH)

    def upper_place(i, j):
        return NBLK - 1 - i, W + i + j

    def lower_place(i, j):
        return j, W - 1 - i - j

    def summed(k, side):
        send_own(k, side).wait_recv()
        send_joined(k, 0, side).wait_recv()

    def inner_sums(k):
        summed(k, None)
        sums(k * EARLY, [(i, W + j - i - 1) for i, j in INNER_PART[k]], ts_in, GI[k])
        tr_in[a, GI[k]:GI[k + 1]] = ts_in[a, GI[k]:GI[k + 1]]
        for r in range(1, AUX):
            send_in(k, r).start()

    def edge_sums(k, side):
        summed(k, side)
        spot, ts = (upper_place, ts_r) if side == "R" else (lower_place, ts_l)
        sums(start_of(k, side), [spot(i, j) for i, j in tiles_of(k, side)], ts, GX[k][0])

        @pl.when(edge(side)[0])
        def _():
            for to in range(AUX):
                send_x(k, side, to).start()

    def place(tr, g0, places):
        for u, (m, e) in enumerate(places):
            g, v = g0 + u // 4, u % 4
            pieces = [tr[source, g, :, v * SL:(v + 1) * SL].astype(jnp.float32) for source in range(AUX)]
            out_ref[m, e] = jnp.concatenate(pieces, axis=1)

    def inner_place(k):
        for r in range(1, AUX):
            send_in(k, r).wait_recv()
        place(tr_in, GI[k], [(j, W - (j - i)) for i, j in INNER_PART[k]])

    def edge_place(k, side):
        @pl.when(has_left if side == "R" else has_right)
        def _():
            for source in range(AUX):
                got_x(k, side, source).wait_recv()

        spot, tr = (lower_place, tr_r) if side == "R" else (upper_place, tr_l)
        place(tr, GX[k][0], [spot(i, j) for i, j in tiles_of(k, side)])

    def tail_to_right(to):
        return pltpu.make_async_remote_copy(
            tail_r.at[to], tail_r_in.at[a], cs.at[3, to], cr.at[3, a],
            device_id={"ao": right, "aux": to}, device_id_type=MESH)

    def tail_to_left(to):
        return pltpu.make_async_remote_copy(
            tail_l.at[to], tail_l_in.at[a], cs.at[3, to], cr.at[3, a],
            device_id={"ao": left, "aux": to}, device_id_type=MESH)

    def tail_from_left(source):
        return pltpu.make_async_remote_copy(
            tail_r.at[source], tail_r_in.at[source], cs.at[3, source], cr.at[3, source],
            device_id={"ao": left, "aux": source}, device_id_type=MESH)

    def tail_from_right(source):
        return pltpu.make_async_remote_copy(
            tail_l.at[source], tail_l_in.at[source], cs.at[3, source], cr.at[3, source],
            device_id={"ao": right, "aux": source}, device_id_type=MESH)

    def tail_out(side, to):
        return tail_to_right(to) if side == "R" else tail_to_left(to)

    def tail_send(side):
        for r in range(1, AUX):
            send_tail(r, side).start()

        @pl.when(edge(side)[0])
        def _():
            for to in range(AUX):
                tail_out(side, to).start()

    def tail_finish(side, other):
        for r in range(1, AUX):
            send_tail(r, side).wait_recv()
        spot = upper_place if side == "R" else lower_place
        for u, (i, j) in enumerate(tiles_of(LAST, side)):
            value = part[a, start_of(LAST, side) + u].astype(jnp.float32)
            for r in range(1, AUX):
                value = value + tail_in[r - 1, u].astype(jnp.float32)
            out_ref[spot(i, j)] = value

        @pl.when(edge(side)[0])
        def _():
            for source in range(AUX):
                (tail_from_left if other == "R" else tail_from_right)(source).wait_recv()

        spot, arrived = (lower_place, tail_r_in) if other == "R" else (upper_place, tail_l_in)
        for u, (i, j) in enumerate(tiles_of(LAST, other)):
            value = arrived[0, u].astype(jnp.float32)
            for source in range(1, AUX):
                value = value + arrived[source, u].astype(jnp.float32)
            out_ref[spot(i, j)] = value

    def by_side(step):
        @pl.when(even)
        def _():
            step("R", "L")

        @pl.when(jnp.logical_not(even))
        def _():
            step("L", "R")

    def fast_step(fast, slow):
        for b in range(3):
            cross(fast, b, False)

    def slow_step(b):
        def step(fast, slow):
            cross(slow, b, True)
            if b < 2:
                alpha(SLOW0 + b, slow)
            else:
                tail_send(slow)
        return step

    by_side(fast_step)
    beta(0, None)
    relay(1)
    by_side(lambda fast, slow: alpha(FAST, fast))
    by_side(slow_step(0))
    relay(2)
    beta(1, None)
    by_side(lambda fast, slow: beta(FAST, fast))
    by_side(slow_step(1))
    by_side(lambda fast, slow: beta(SLOW0, slow))
    inner_sums(0)
    inner_sums(1)
    by_side(lambda fast, slow: beta(SLOW1, slow))
    by_side(lambda fast, slow: edge_sums(FAST, fast))
    by_side(lambda fast, slow: edge_sums(SLOW0, slow))
    by_side(slow_step(2))
    by_side(lambda fast, slow: edge_sums(SLOW1, slow))
    inner_place(0)
    inner_place(1)
    by_side(lambda fast, slow: edge_place(FAST, slow))
    by_side(lambda fast, slow: edge_place(SLOW0, fast))
    by_side(lambda fast, slow: edge_place(SLOW1, fast))
    by_side(lambda fast, slow: tail_finish(slow, fast))

    def drain(fast, slow):
        for k, side in enumerate((None, None, fast, slow, slow)):
            send_own(k, side).wait_send()

            @pl.when(outer)
            def _():
                send_far(k, side).wait_send()

            @pl.when(jnp.logical_not(outer))
            def _():
                for h in range(2):
                    send_joined(k, h, side).wait_send()

        for r in range(1, AUX):
            send_tail(r, slow).wait_send()
        for k, side in ((FAST, fast), (SLOW0, slow), (SLOW1, slow)):
            @pl.when(edge(side)[0])
            def _():
                for to in range(AUX):
                    send_x(k, side, to).wait_send()

        @pl.when(edge(slow)[0])
        def _():
            for to in range(AUX):
                tail_out(slow, to).wait_send()

    by_side(drain)
    for r in range(1, AUX):
        for k in range(2):
            send_in(k, r).wait_send()

    @pl.when(has_right)
    def _():
        mask_copy.wait_send()

    for b in range(3):
        @pl.when(near_right)
        def _():
            to_right(b).wait_send()

        @pl.when(near_left)
        def _():
            to_left(b).wait_send()

        @pl.when(at_seam)
        def _():
            for p in range(PATHS):
                seam_out(b, p).wait_send()

        for p in range(1, PATHS):
            @pl.when(is_relay(p))
            def _():
                relay_out(b, p).wait_send()


def body(half_transformed, pair_mask):
    flat = half_transformed.reshape(-1, NBLK * BS)
    rows = flat.shape[0]
    bf16 = jnp.bfloat16
    dma = pltpu.SemaphoreType.DMA
    return pl.pallas_call(
        kernel,
        out_shape=jax.ShapeDtypeStruct((NBLK, 2 * W, SL, BS), jnp.float32),
        in_specs=[pl.BlockSpec(memory_space=pl.ANY)] * 2,
        out_specs=pl.BlockSpec(memory_space=pltpu.VMEM),
        scratch_shapes=[
            pltpu.VMEM((rows, NBLK * BS), bf16),
            pltpu.VMEM((rows // KC, NBLK * BS, KC), bf16),
            pltpu.VMEM((3, rows, 2 * BS), bf16),
            pltpu.VMEM((3, max(CUTS[p + 1] - CUTS[p] for p in range(1, PATHS)), BS), bf16),
            pltpu.VMEM((sum(INNER_M) * BS, 2 * BS), jnp.float32),
            pltpu.VMEM((AUX, N_ALL, SL, BS), bf16),
            pltpu.VMEM((N_ALL, SL, BS), bf16),
            pltpu.VMEM((2, N_ALL, SL, BS), bf16),
            pltpu.VMEM((2, N_ALL, SL, BS), bf16),
            pltpu.VMEM((N_ALL, SL, BS), bf16),
            pltpu.VMEM((AUX - 1, len(RIGHT[2]), SL, BS), bf16),
            pltpu.VMEM((AUX, GI[2], SL, BS), bf16),
            pltpu.VMEM((AUX, 3, SL, BS), bf16),
            pltpu.VMEM((AUX, 3, SL, BS), bf16),
            pltpu.VMEM((AUX, GI[2], SL, BS), bf16),
            pltpu.VMEM((AUX, 3, SL, BS), bf16),
            pltpu.VMEM((AUX, 3, SL, BS), bf16),
            pltpu.VMEM((AUX, len(RIGHT[2]), SL, BS), bf16),
            pltpu.VMEM((AUX, len(LEFT[2]), SL, BS), bf16),
            pltpu.VMEM((AUX, len(RIGHT[2]), SL, BS), bf16),
            pltpu.VMEM((AUX, len(LEFT[2]), SL, BS), bf16),
            pltpu.VMEM((NBLK, W), jnp.int32),
            pltpu.VMEM((NBLK, W), jnp.int32),
            dma((rows // KC,)), dma,
            dma((2, 3)), dma((2, 3)),
            dma((PATHS, 3)), dma((PATHS, 3)), dma((3,)), dma((3,)),
            dma, dma,
            dma((5,)), dma((5,)),
            dma((5,)), dma((5,)),
            dma((5, 2)), dma((5,)),
            dma((AUX - 1,)), dma((AUX - 1,)),
            dma((2, AUX - 1)), dma((2, AUX - 1)),
            dma((4, AUX)), dma((4, AUX)),
        ],
        compiler_params=pltpu.CompilerParams(
            collective_id=0, has_side_effects=True, vmem_limit_bytes=48 << 20),
        cost_estimate=pl.CostEstimate(flops=8 << 30, bytes_accessed=16 << 20, transcendentals=0),
    )(flat, pair_mask)


def solution(mesh):
    return jax.shard_map(
        body,
        mesh=mesh,
        in_specs=(P("aux", None, "ao"), P("ao", None)),
        out_specs=P("ao", None, "aux", None),
        check_vma=False,
    )
```

time: 67 us -> 64.6 us (0.964)
  Pallas kernels: 64.7 us -> 62.7 us
    pallas_call x1, Pallas kernels: 64.7 us -> 62.7 us  [body(): pl.pallas_call(kernel, out_shape=jax.ShapeDtypeStruct((NBLK, 2 * W, SL, B...]
where the time goes in v5:
time: 64.6 us; the launch traced here: 64.5 us
  Pallas kernels  62.7 us (97%)
  local copies, waits for them, and re-layouts  1.83 us (3%)
    pallas_call x1, Pallas kernels, body(): pl.pallas_call(kernel, out_shape=jax.ShapeDtypeStruct((NBLK, 2 * W, SL, B...  62.7 us
    unnamed x3, local copies, waits for them, and re-layouts  1.83 us

profile of v5, /device:TPU:31, one launch (start us, length us, event | category | flops | bytes accessed | tf_op | source)
XLA Modules:
  0.0 64.5 jit_solution(4771147166083571708)
XLA Ops:
  0.0 0.0 copy-start
  0.0 0.7 %copy-done = s32[8,6]{1,0:T(8,128)S(1)} copy-done((s32[8,6]{1,0:T(8,128)S(1)}, s32[8,6]{1,0:T(8,128)}, u32[]{:S(2)}) %copy-start) | copy-done | bytes 216
  0.7 62.7 %shard_map.28 = f32[8,12,32,128]{3,2,1,0:T(8,128)S(1)} custom-call(bf16[4096,1024]{1,0:T(8,128)(2,1)} %bitcast.1, s32[8,6]{1,0:T(8,128)S(1)} %copy-done), custom_call_target="tpu_custom_call" | custom-call | flops 8589934592 | bytes 16777216 | tf_op jit(solution)/shard_map/pallas_call | solution.py:587
  63.4 1.1 %copy.4 = f32[8,12,32,128]{3,2,1,0:T(8,128)} copy(f32[8,12,32,128]{3,2,1,0:T(8,128)S(1)} %shard_map.28) | data formatting | bytes 3145728
Async XLA Ops:
  0.0 0.7 %copy-start = (s32[8,6]{1,0:T(8,128)S(1)}, s32[8,6]{1,0:T(8,128)}, u32[]{:S(2)}) copy-start(s32[8,6]{1,0:T(8,128)} %mask_hbm.1) | copy-start | bytes 580

commit v6 on v5

--- a/solution.py
+++ b/solution.py
@@ -179,25 +179,25 @@
     mask_copy = pltpu.make_async_remote_copy(
         mask_own, mask_prev, ms, mr, device_id={"ao": right}, device_id_type=MESH)
 
+    for b in range(3):
+        @pl.when(at_seam)
+        def _():
+            for p in (1, 2, 4, 3, 0):
+                seam_out(b, p).start()
+
+        @pl.when(near_left)
+        def _():
+            to_left(b).start()
+
+        @pl.when(near_right)
+        def _():
+            to_right(b).start()
+
     mask_load.wait()
 
     @pl.when(has_right)
     def _():
         mask_copy.start()
-
-    for b in range(3):
-        @pl.when(near_left)
-        def _():
-            to_left(b).start()
-
-        @pl.when(near_right)
-        def _():
-            to_right(b).start()
-
-        @pl.when(at_seam)
-        def _():
-            for p in (1, 2, 4, 3, 0):
-                seam_out(b, p).start()
 
     @pl.when(jnp.logical_not(has_left))
     def _():

time: 64.6 us -> 72.4 us (1.12)
  Pallas kernels: 62.7 us -> 70.4 us
    pallas_call x1, Pallas kernels: 62.7 us -> 70.4 us  [body(): pl.pallas_call(kernel, out_shape=jax.ShapeDtypeStruct((NBLK, 2 * W, SL, B...]
where the time goes in v6:
time: 72.4 us; the launch traced here: 72.3 us
  Pallas kernels  70.4 us (97%)
  local copies, waits for them, and re-layouts  1.83 us (3%)
    pallas_call x1, Pallas kernels, body(): pl.pallas_call(kernel, out_shape=jax.ShapeDtypeStruct((NBLK, 2 * W, SL, B...  70.4 us
    unnamed x3, local copies, waits for them, and re-layouts  1.83 us

profile of v6, /device:TPU:31, one launch (start us, length us, event | category | flops | bytes accessed | tf_op | source)
XLA Modules:
  0.0 72.3 jit_solution(5446146602199936788)
XLA Ops:
  0.0 0.0 copy-start
  0.0 0.7 copy-done
  0.7 70.4 %shard_map.28 = f32[8,12,32,128]{3,2,1,0:T(8,128)S(1)} custom-call(bf16[4096,1024]{1,0:T(8,128)(2,1)} %bitcast.1, s32[8,6]{1,0:T(8,128)S(1)} %copy-done), custom_call_target="tpu_custom_call" | custom-call | flops 8589934592 | bytes 16777216 | tf_op jit(solution)/shard_map/pallas_call | solution.py:587
  71.1 1.1 %copy.4 = f32[8,12,32,128]{3,2,1,0:T(8,128)} copy(f32[8,12,32,128]{3,2,1,0:T(8,128)S(1)} %shard_map.28) | data formatting | bytes 3145728
Async XLA Ops:
  0.0 0.7 copy-start
